TPU v7x, 256 devices: a whole 4x4x8 slice. The times are simulated.
256 devices in a mesh: pipe: 8 (over z_lo, y), expert: 16 (over z_hi, x), dp: 2 (over core).
Axes of the slice: x: 4, y: 4, z: 8 (z_hi: 4, z_lo: 2; z = z_hi * 2 + z_lo), core: 2. Of those that a mesh axis runs over, the one named last changes fastest.
Arguments:
- act_in: bfloat16 [8, 1024, 3584], P('pipe', ('expert', 'dp')), may hold values from -6 to 6
- fresh_in: bfloat16 [1024, 3584], P(('expert', 'dp')), may hold values from -6 to 6
- grad_in: bfloat16 [8, 1024, 3584], P('pipe', ('expert', 'dp')), may hold values from -6 to 6
- fresh_grad: bfloat16 [1024, 3584], P(('expert', 'dp')), may hold values from -6 to 6
- saved_input: bfloat16 [2, 8, 1024, 3584], P(None, 'pipe', ('expert', 'dp')), may hold values from -6 to 6
- expert_ids: int32 [8, 4, 1024, 1], P('pipe', None, ('expert', 'dp')), may hold values from 0 to 7, as said below
- slot_ids: int32 [8, 4, 1024, 1], P('pipe', None, ('expert', 'dp')), may hold values from 0 to 5, as said below
- gates: float32 [8, 4, 1024, 1], P('pipe', None, ('expert', 'dp')), may hold values from 0.3 to 2
- up_weight: bfloat16 [8, 3584, 8192], P('pipe', 'dp', 'expert'), may hold values from -0.09375 to 0.09375
- down_weight: bfloat16 [8, 8192, 3584], P('pipe', 'expert', 'dp'), may hold values from -0.1875 to 0.1875
Outputs:
- activations_out: bfloat16 [2, 8, 1024, 3584], P(None, 'pipe', ('expert', 'dp'))
- input_grads: bfloat16 [2, 8, 1024, 3584], P(None, 'pipe', ('expert', 'dp'))
- up_grad: bfloat16 [8, 3584, 8192], P('pipe', 'dp', 'expert')
- down_grad: bfloat16 [8, 8192, 3584], P('pipe', 'expert', 'dp')
Inputs may be any that keep to these rules, and one draw needn't show every extreme that they name: `expert_ids`: each token names exactly one expert. Within one aligned block of 32 tokens, for one section and pass, no expert is named more than 6 times, and some expert is named exactly 6 times. `slot_ids`: within one aligned block of 32 tokens, for one section, pass and expert, the tokens naming that expert hold the slots 0, 1, 2 and onward in token order.
All inputs are finite; a program needn't handle non-finite values.
Results may differ from a plain program's by a relative error of at most 0.0065.
Values may be sent and summed in bfloat16 or wider, within the bound.
A program may use at most 128 MiB of HBM per device.

v0:
```python
import jax
import jax.numpy as jnp
from jax import lax
from jax.sharding import PartitionSpec as P

HALVES = 2


def shifted(x, axis, by):
    length = lax.axis_size(axis)
    pairs = [(i, i + by) for i in range(length) if 0 <= i + by < length]
    return lax.ppermute(x, axis, pairs)


def silu_slope(values):
    logistic = jax.nn.sigmoid(values)
    return logistic * (1.0 + values * (1.0 - logistic))


def times_rows(left, right):
    return lax.dot_general(
        left, right, (((1,), (1,)), ((), ())), preferred_element_type=jnp.float32
    )


def over_slots(left, right):
    return lax.dot_general(
        left, right, (((0,), (0,)), ((), ())), preferred_element_type=jnp.float32
    )


def per_device(
    act_in,
    fresh_in,
    grad_in,
    fresh_grad,
    saved_input,
    expert_ids,
    slot_ids,
    gates,
    up_weight,
    down_weight,
):
    sections = lax.axis_size("pipe")
    section_index = lax.axis_index("pipe")
    owners = lax.axis_size("expert")
    experts = owners // HALVES
    tokens_here = act_in.shape[1]
    features = act_in.shape[2]
    chosen_count = expert_ids.shape[3]
    capacity = 2 * ((9 * chosen_count * tokens_here + 16 * experts - 1) // (16 * experts))
    up_full, down_full = (
        lax.all_gather(up_weight[0], "dp", axis=0, tiled=True),
        lax.all_gather(down_weight[0], "dp", axis=1, tiled=True),
    )

    def tables(pass_index):
        chosen = expert_ids[0, pass_index]
        position = (chosen * capacity + slot_ids[0, pass_index]).reshape(-1)
        source = jnp.repeat(jnp.arange(tokens_here, dtype=jnp.int32), chosen_count)
        source_table = (
            jnp.full((experts * capacity,), tokens_here, dtype=jnp.int32).at[position].set(source)
        )
        return (position, source_table)

    def padded_rows(values, source_table):
        padded = jnp.concatenate([values, jnp.zeros((1, features), values.dtype)], axis=0)
        return padded[source_table]

    def deliver(stacked):
        sending = jnp.repeat(stacked, HALVES, axis=1)
        return lax.all_to_all(sending, "expert", split_axis=1, concat_axis=1, tiled=True)

    def collect(partial_value):
        returned = lax.all_to_all(partial_value, "expert", split_axis=0, concat_axis=0, tiled=True)
        return (
            returned.reshape(experts, HALVES, capacity, features)
            .astype(jnp.float32)
            .sum(axis=1)
            .astype(jnp.bfloat16)
        )

    def mix_back(values, position, weights, expert_out):
        picked = (
            expert_out.reshape(-1, features)[position]
            .reshape(tokens_here, chosen_count, features)
            .astype(jnp.float32)
        )
        return (values.astype(jnp.float32) + jnp.sum(weights[:, :, None] * picked, axis=1)).astype(
            jnp.bfloat16
        )

    def forward_pass(values, pass_index):
        position, source_table = tables(pass_index)
        slot_rows = padded_rows(values, source_table).reshape(1, experts, capacity, features)
        arrived = deliver(slot_rows)[0].reshape(-1, features)
        hidden = jax.nn.silu(jnp.dot(arrived, up_full, preferred_element_type=jnp.float32)).astype(
            jnp.bfloat16
        )
        partial_value = jnp.dot(hidden, down_full, preferred_element_type=jnp.float32).astype(
            jnp.bfloat16
        )
        return mix_back(
            values,
            position,
            gates[0, pass_index],
            collect(partial_value.reshape(owners, capacity, features)),
        )

    def backward_pass(values, upstream, pass_index):
        position, source_table = tables(pass_index)
        gate_table = (
            jnp.zeros((experts * capacity,), jnp.float32)
            .at[position]
            .set(gates[0, pass_index].reshape(-1))
        )
        slot_grads = (
            gate_table[:, None] * padded_rows(upstream, source_table).astype(jnp.float32)
        ).astype(jnp.bfloat16)
        stacked = jnp.stack([padded_rows(values, source_table), slot_grads]).reshape(
            2, experts, capacity, features
        )
        arrived = deliver(stacked)
        inputs = arrived[0].reshape(-1, features)
        grads_here = arrived[1].reshape(-1, features)
        projected = jnp.dot(inputs, up_full, preferred_element_type=jnp.float32)
        hidden = jax.nn.silu(projected).astype(jnp.bfloat16)
        hidden_grad = times_rows(grads_here, down_full)
        pre_grad = (hidden_grad * silu_slope(projected)).astype(jnp.bfloat16)
        partial_value = times_rows(pre_grad, up_full).astype(jnp.bfloat16)
        unit_gates = jnp.ones_like(gates[0, pass_index])
        input_grad = mix_back(
            upstream,
            position,
            unit_gates,
            collect(partial_value.reshape(owners, capacity, features)),
        )
        return (input_grad, (inputs, grads_here, hidden, pre_grad))

    first_out = forward_pass(act_in[0], 0)
    first_back, first_parts = backward_pass(saved_input[0, 0], grad_in[0], 2)
    from_below = shifted(first_out, "pipe", 1)
    from_above = shifted(first_back, "pipe", -1)
    second_in = jnp.where(section_index == 0, fresh_in, from_below)
    second_upstream = jnp.where(section_index == sections - 1, fresh_grad, from_above)
    second_out = forward_pass(second_in, 1)
    second_back, second_parts = backward_pass(saved_input[1, 0], second_upstream, 3)
    joined = [jnp.concatenate([first_parts[item], second_parts[item]], axis=0) for item in range(4)]
    up_local = over_slots(joined[0], joined[3])
    down_local = over_slots(joined[2], joined[1])
    up_total, down_total = (
        lax.psum_scatter(up_local, "dp", scatter_dimension=0, tiled=True),
        lax.psum_scatter(down_local, "dp", scatter_dimension=1, tiled=True),
    )
    activations_out = jnp.stack([first_out, second_out])[:, None]
    input_grads = jnp.stack([first_back, second_back])[:, None]
    return (
        activations_out,
        input_grads,
        up_total.astype(jnp.bfloat16)[None],
        down_total.astype(jnp.bfloat16)[None],
    )


def solution(mesh):
    in_specs = (
        P("pipe", ("expert", "dp"), None),
        P(("expert", "dp"), None),
        P("pipe", ("expert", "dp"), None),
        P(("expert", "dp"), None),
        P(None, "pipe", ("expert", "dp"), None),
        P("pipe", None, ("expert", "dp"), None),
        P("pipe", None, ("expert", "dp"), None),
        P("pipe", None, ("expert", "dp"), None),
        P("pipe", "dp", "expert"),
        P("pipe", "expert", "dp"),
    )
    out_specs = (
        P(None, "pipe", ("expert", "dp"), None),
        P(None, "pipe", ("expert", "dp"), None),
        P("pipe", "dp", "expert"),
        P("pipe", "expert", "dp"),
    )
    return jax.shard_map(
        per_device, mesh=mesh, in_specs=in_specs, out_specs=out_specs, check_vma=False
    )
```

profile of v0, /device:TPU:32, one launch (start us, length us, event | category | flops | bytes accessed | tf_op | source)
XLA Modules:
  0.0 366.3 jit_solution(7999210482760572741)
XLA Ops:
  15.0 46.3 %all_to_all.40 = bf16[2,16,6,3584]{3,0,2,1:T(2,128)(2,1)S(1)} all-to-all(bf16[2,16,6,3584]{3,0,2,1:T(2,128)(2,1)S(1)} %bitcast.134), channel_id=1, replica_groups=mesh['pipe'=8,'expert'=16,'dp'=2] {'expert'}, dimensions={1} | all-to-all | bytes 2752512 | tf_op jit(solution)/shard_map/all_to_all | solution.py:72
  61.3 6.1 %slice_reduce_fusion.2 = (bf16[16,6,3584]{2,1,0:T(8,128)(2,1)S(1)}, bf16[16,6,3584]{2,1,0:T(8,128)(2,1)S(1)}) fusion(bf16[2,16,6,3584]{3,0,2,1:T(2,128)(2,1)S(1)} %all_to_all.40), kind=kLoop, calls=%fused_computation.40 | loop fusion | bytes 2752512 | tf_op jit(solution)/shard_map/slice | solution.py:124
  67.8 3.4 multiply_convert_fusion.3
  71.3 3.4 fusion.33
  77.2 3.8 %all-to-all-start.5 = ((bf16[16,6,3584]{2,1,0:T(8,128)(2,1)}), bf16[16,6,3584]{2,1,0:T(8,128)(2,1)S(1)}, u32[]{:S(2)}, u32[]{:S(2)}) async-start(bf16[16,6,3584]{2,1,0:T(8,128)(2,1)} %reshape.386), calls=%async_computation.5 | async-start | bytes 1835008 | tf_op jit(solution)/shard_map/all_to_all | solution.py:75
  82.5 18.4 %all-to-all-done.5 = bf16[16,6,3584]{2,1,0:T(8,128)(2,1)S(1)} async-done(((bf16[16,6,3584]{2,1,0:T(8,128)(2,1)}), bf16[16,6,3584]{2,1,0:T(8,128)(2,1)S(1)}, u32[]{:S(2)}, u32[]{:S(2)}) %all-to-all-start.5) | async-done | bytes 688160 | tf_op jit(solution)/shard_map/all_to_all | solution.py:75
  102.0 12.3 %collective-permute-start.1 = (bf16[32,3584]{1,0:T(8,128)(2,1)S(1)}, bf16[32,3584]{1,0:T(8,128)(2,1)S(1)}, u32[]{:S(2)}, u32[]{:S(2)}) collective-permute-start(bf16[32,3584]{1,0:T(8,128)(2,1)S(1)} %fusion.43), channel_id=1, source_target_pairs={{32,0},{64,32},{96,64},{128,96},{160,128},{192,160},{224,192},{33,... | collective-permute-start | bytes 688136 | tf_op jit(solution)/shard_map/ppermute | solution.py:12
  115.2 2.4 collective-permute-done.1
  117.6 1.5 gather_fusion.8
  122.0 40.6 %all_to_all.41 = bf16[2,16,6,3584]{3,0,2,1:T(2,128)(2,1)S(1)} all-to-all(bf16[2,16,6,3584]{3,0,2,1:T(2,128)(2,1)S(1)} %bitcast.135), channel_id=1, replica_groups=mesh['pipe'=8,'expert'=16,'dp'=2] {'expert'}, dimensions={1} | all-to-all | bytes 2752512 | tf_op jit(solution)/shard_map/all_to_all | solution.py:72
  162.5 7.2 %slice_reduce_fusion = (bf16[16,6,3584]{2,1,0:T(8,128)(2,1)}, bf16[16,6,3584]{2,1,0:T(8,128)(2,1)}) fusion(bf16[2,16,6,3584]{3,0,2,1:T(2,128)(2,1)S(1)} %all_to_all.41), kind=kLoop, calls=%fused_computation.38 | loop fusion | bytes 2752512 | tf_op jit(solution)/shard_map/slice | solution.py:124
  169.7 1.4 reshape_squeeze.31
  171.1 1.4 reshape_squeeze.30
  172.5 3.6 multiply_convert_fusion.2
  177.3 4.1 %fusion.16 = f32[3584,512]{1,0:T(8,128)} fusion(bf16[96,3584]{1,0:T(8,128)(2,1)S(1)} %reshape_squeeze.31, bf16[96,3584]{1,0:T(8,128)(2,1)S(1)} %reshape_squeeze.28, bf16[96,512]{1,0:T(8,128)(2,1)S(1)} %fusion.30, bf16[96,512]{1,0:T(8,128)(2,1)S(1)} %copy-done.6), kind=kOutput, calls=%fused_computation.42 | convolution fusion | flops 707788800 | bytes 8912896 | tf_op jit(solution)/shard_map/dot_general | solution.py:27
  182.4 4.1 %fusion.20 = f32[512,3584]{1,0:T(8,128)} fusion(bf16[96,3584]{1,0:T(8,128)(2,1)S(1)} %reshape_squeeze.30, bf16[96,3584]{1,0:T(8,128)(2,1)S(1)} %reshape_squeeze.27, bf16[96,512]{1,0:T(8,128)(2,1)S(1)} %copy-done.9, bf16[96,512]{1,0:T(8,128)(2,1)S(1)} %copy-done.8), kind=kOutput, calls=%fused_computation.46 | convolution fusion | flops 707788800 | bytes 8912896 | tf_op jit(solution)/shard_map/dot_general | solution.py:27
  189.3 25.9 %all_to_all.42 = bf16[1,16,6,3584]{3,2,0,1:T(8,128)(2,1)S(1)} all-to-all(bf16[1,16,6,3584]{3,2,0,1:T(8,128)(2,1)S(1)} %bitcast.136), channel_id=1, replica_groups=mesh['pipe'=8,'expert'=16,'dp'=2] {'expert'}, dimensions={1} | all-to-all | bytes 1376256 | tf_op jit(solution)/shard_map/all_to_all | solution.py:72
  215.4 5.7 %convolution_convert_fusion.3 = bf16[96,3584]{1,0:T(8,128)(2,1)S(1)} fusion(bf16[1,512,3584]{2,1,0:T(8,128)(2,1)} %all-gather.7.cloned.1.call-done, bf16[96,3584]{1,0:T(8,128)(2,1)S(1)} %reshape_squeeze.24, bf16[1,3584,512]{2,1,0:T(8,128)(2,1)} %all-gather.5.cloned.1.call-done), kind=kOutput, calls=%fused_computation.19 | convolution fusion | flops 705232896 | bytes 8716288 | tf_op jit(solution)/shard_map/dot_general | solution.py:100
  222.3 6.6 %all-to-all-start.1 = ((bf16[16,6,3584]{2,1,0:T(8,128)(2,1)}), bf16[16,6,3584]{2,1,0:T(8,128)(2,1)S(1)}, u32[]{:S(2)}, u32[]{:S(2)}) async-start(bf16[16,6,3584]{2,1,0:T(8,128)(2,1)} %reshape.378), calls=%async_computation.1 | async-start | bytes 1835008 | tf_op jit(solution)/shard_map/all_to_all | solution.py:75
  229.6 16.4 %all-to-all-done.1 = bf16[16,6,3584]{2,1,0:T(8,128)(2,1)S(1)} async-done(((bf16[16,6,3584]{2,1,0:T(8,128)(2,1)}), bf16[16,6,3584]{2,1,0:T(8,128)(2,1)S(1)}, u32[]{:S(2)}, u32[]{:S(2)}) %all-to-all-start.1) | async-done | bytes 688160 | tf_op jit(solution)/shard_map/all_to_all | solution.py:75
  247.2 1.9 collective-permute-start
  249.1 8.1 %collective-permute-done = bf16[32,3584]{1,0:T(8,128)(2,1)S(1)} collective-permute-done((bf16[32,3584]{1,0:T(8,128)(2,1)S(1)}, bf16[32,3584]{1,0:T(8,128)(2,1)S(1)}, u32[]{:S(2)}, u32[]{:S(2)}) %collective-permute-start) | collective-permute-done | bytes 229408 | tf_op jit(solution)/shard_map/ppermute | solution.py:12
  259.1 7.3 %all-to-all-start.2 = ((bf16[1,16,6,3584]{3,2,0,1:T(8,128)(2,1)}), bf16[1,16,6,3584]{3,2,0,1:T(8,128)(2,1)S(1)}, u32[]{:S(2)}, u32[]{:S(2)}) async-start(bf16[1,16,6,3584]{3,2,0,1:T(8,128)(2,1)} %bitcast.12), calls=%async_computation.2 | async-start | bytes 1835008 | tf_op jit(solution)/shard_map/all_to_all | solution.py:72
  266.5 22.5 %all-to-all-done.2 = bf16[1,16,6,3584]{3,2,0,1:T(8,128)(2,1)S(1)} async-done(((bf16[1,16,6,3584]{3,2,0,1:T(8,128)(2,1)}), bf16[1,16,6,3584]{3,2,0,1:T(8,128)(2,1)S(1)}, u32[]{:S(2)}, u32[]{:S(2)}) %all-to-all-start.2) | async-done | bytes 688160 | tf_op jit(solution)/shard_map/all_to_all | solution.py:72
  289.2 4.6 %convolution_convert_fusion.2 = bf16[96,3584]{1,0:T(8,128)(2,1)S(1)} fusion(bf16[1,512,3584]{2,1,0:T(8,128)(2,1)} %all-gather.7.cloned.1.call-done, bf16[96,3584]{1,0:T(8,128)(2,1)S(1)} %reshape_squeeze.25, bf16[1,3584,512]{2,1,0:T(8,128)(2,1)} %all-gather.5.cloned.1.call-done), kind=kOutput, calls=%fused_computation.18 | convolution fusion | flops 705232896 | bytes 8716288 | tf_op jit(solution)/shard_map/dot_general | solution.py:100
  294.9 3.8 %all-to-all-start.3 = ((bf16[16,6,3584]{2,1,0:T(8,128)(2,1)}), bf16[16,6,3584]{2,1,0:T(8,128)(2,1)S(1)}, u32[]{:S(2)}, u32[]{:S(2)}) async-start(bf16[16,6,3584]{2,1,0:T(8,128)(2,1)} %reshape.382), calls=%async_computation.3 | async-start | bytes 1835008 | tf_op jit(solution)/shard_map/all_to_all | solution.py:75
  298.9 25.0 %all-to-all-done.3 = bf16[16,6,3584]{2,1,0:T(8,128)(2,1)S(1)} async-done(((bf16[16,6,3584]{2,1,0:T(8,128)(2,1)}), bf16[16,6,3584]{2,1,0:T(8,128)(2,1)S(1)}, u32[]{:S(2)}, u32[]{:S(2)}) %all-to-all-start.3) | async-done | bytes 688160 | tf_op jit(solution)/shard_map/all_to_all | solution.py:75
  324.2 3.3 convolution_convert_fusion
  328.7 4.4 %all-to-all-start.7 = ((bf16[16,6,3584]{2,1,0:T(8,128)(2,1)}), bf16[16,6,3584]{2,1,0:T(8,128)(2,1)S(1)}, u32[]{:S(2)}, u32[]{:S(2)}) async-start(bf16[16,6,3584]{2,1,0:T(8,128)(2,1)} %reshape.390), calls=%async_computation.7 | async-start | bytes 1835008 | tf_op jit(solution)/shard_map/all_to_all | solution.py:75
  334.7 16.2 %all-to-all-done.7 = bf16[16,6,3584]{2,1,0:T(8,128)(2,1)S(1)} async-done(((bf16[16,6,3584]{2,1,0:T(8,128)(2,1)}), bf16[16,6,3584]{2,1,0:T(8,128)(2,1)S(1)}, u32[]{:S(2)}, u32[]{:S(2)}) %all-to-all-start.7) | async-done | bytes 688160 | tf_op jit(solution)/shard_map/all_to_all | solution.py:75
  352.8 3.5 convert_bitcast_fusion.1
  356.3 3.4 convert_bitcast_fusion
  (134 shorter events, 33.3 us)
Async XLA Ops:
  7.2 1.5 copy-start.12
  7.2 1.5 copy-start.13
  7.2 2.7 copy-start.17
  7.2 3.5 copy-start.7
  7.2 4.2 %copy-start.3 = (bf16[1,32,3584]{2,1,0:T(8,128)(2,1)S(1)}, bf16[1,32,3584]{2,1,0:T(8,128)(2,1)}, u32[]{:S(2)}) copy-start(bf16[1,32,3584]{2,1,0:T(8,128)(2,1)} %param.12) | copy-start | bytes 688132
  7.2 60.6 %all-gather.5.cloned.1.call-start = ((), (), s32[]{:S(2)}) async-start(), calls=%async_computation.12 | async-start | bytes 5505024 | tf_op jit(solution)/shard_map/all_gather | solution.py:53
  8.0 63.3 %all-gather.7.cloned.1.call-start = ((), (), s32[]{:S(2)}) async-start(), calls=%async_computation.13 | async-start | bytes 5505024 | tf_op jit(solution)/shard_map/all_gather | solution.py:54
  9.2 219.7 %copy-start.14 = (s32[32]{0:T(128)}, s32[32]{0:T(128)S(1)}, u32[]{:S(2)}) copy-start(s32[32]{0:T(128)S(1)} %get-tuple-element.23) | copy-start | bytes 388
  71.3 3.4 copy-start
  74.7 2.4 copy-start.5
  74.7 7.7 %copy-start.4 = (bf16[32,3584]{1,0:T(8,128)(2,1)S(1)}, bf16[32,3584]{1,0:T(8,128)(2,1)}, u32[]{:S(2)}) copy-start(bf16[32,3584]{1,0:T(8,128)(2,1)} %get-tuple-element.20) | copy-start | bytes 688132
  77.2 23.7 %all-to-all-start.5 = ((bf16[16,6,3584]{2,1,0:T(8,128)(2,1)}), bf16[16,6,3584]{2,1,0:T(8,128)(2,1)S(1)}, u32[]{:S(2)}, u32[]{:S(2)}) async-start(bf16[16,6,3584]{2,1,0:T(8,128)(2,1)} %reshape.386), calls=%async_computation.5 | async-start | bytes 1835008 | tf_op jit(solution)/shard_map/all_to_all | solution.py:75
  80.9 271.8 %reduce-scatter.3.cloned.1.call-start = ((), (), s32[]{:S(2)}) async-start(), calls=%async_computation.10 | async-start | bytes 11010048 | tf_op jit(solution)/shard_map/reduce_scatter | solution.py:152
  101.1 16.5 %copy-start.10 = (bf16[32,3584]{1,0:T(8,128)(2,1)S(1)}, bf16[32,3584]{1,0:T(8,128)(2,1)}, u32[]{:S(2)}) copy-start(bf16[32,3584]{1,0:T(8,128)(2,1)} %param.13) | copy-start | bytes 688132
  102.0 15.6 %collective-permute-start.1 = (bf16[32,3584]{1,0:T(8,128)(2,1)S(1)}, bf16[32,3584]{1,0:T(8,128)(2,1)S(1)}, u32[]{:S(2)}, u32[]{:S(2)}) collective-permute-start(bf16[32,3584]{1,0:T(8,128)(2,1)S(1)} %fusion.43), channel_id=1, source_target_pairs={{32,0},{64,32},{96,64},{128,96},{160,128},{192,160},{224,192},{33,... | collective-permute-start | bytes 688136 | tf_op jit(solution)/shard_map/ppermute | solution.py:12
  172.5 3.6 copy-start.1
  172.5 4.8 %copy-start.6 = (bf16[96,512]{1,0:T(8,128)(2,1)S(1)}, bf16[96,512]{1,0:T(8,128)(2,1)}, u32[]{:S(2)}) copy-start(bf16[96,512]{1,0:T(8,128)(2,1)} %copy-done.5) | copy-start | bytes 294916
  181.5 0.9 copy-start.8
  181.5 0.9 copy-start.9
  181.5 174.8 %reduce-scatter.5.cloned.1.call-start = ((), (), s32[]{:S(2)}) async-start(), calls=%async_computation.11 | async-start | bytes 11010048 | tf_op jit(solution)/shard_map/reduce_scatter | solution.py:153
  186.5 1.0 copy-start.2
  186.6 1.1 copy-start.16
  222.3 34.9 %copy-start.11 = (bf16[32,3584]{1,0:T(8,128)(2,1)S(1)}, bf16[32,3584]{1,0:T(8,128)(2,1)}, u32[]{:S(2)}) copy-start(bf16[32,3584]{1,0:T(8,128)(2,1)} %param.11) | copy-start | bytes 688132
  222.3 23.7 %all-to-all-start.1 = ((bf16[16,6,3584]{2,1,0:T(8,128)(2,1)}), bf16[16,6,3584]{2,1,0:T(8,128)(2,1)S(1)}, u32[]{:S(2)}, u32[]{:S(2)}) async-start(bf16[16,6,3584]{2,1,0:T(8,128)(2,1)} %reshape.378), calls=%async_computation.1 | async-start | bytes 1835008 | tf_op jit(solution)/shard_map/all_to_all | solution.py:75
  247.2 10.0 %collective-permute-start = (bf16[32,3584]{1,0:T(8,128)(2,1)S(1)}, bf16[32,3584]{1,0:T(8,128)(2,1)S(1)}, u32[]{:S(2)}, u32[]{:S(2)}) collective-permute-start(bf16[32,3584]{1,0:T(8,128)(2,1)S(1)} %fusion.40), channel_id=1, source_target_pairs={{0,32},{32,64},{64,96},{96,128},{128,160},{160,192},{192,224},{1,3... | collective-permute-start | bytes 688136 | tf_op jit(solution)/shard_map/ppermute | solution.py:12
  257.3 9.2 %copy-start.15 = (s32[32]{0:T(128)S(1)}, s32[32]{0:T(128)}, u32[]{:S(2)}) copy-start(s32[32]{0:T(128)} %copy-done.14) | copy-start | bytes 388
  259.1 29.8 %all-to-all-start.2 = ((bf16[1,16,6,3584]{3,2,0,1:T(8,128)(2,1)}), bf16[1,16,6,3584]{3,2,0,1:T(8,128)(2,1)S(1)}, u32[]{:S(2)}, u32[]{:S(2)}) async-start(bf16[1,16,6,3584]{3,2,0,1:T(8,128)(2,1)} %bitcast.12), calls=%async_computation.2 | async-start | bytes 1835008 | tf_op jit(solution)/shard_map/all_to_all | solution.py:72
  294.9 29.0 %all-to-all-start.3 = ((bf16[16,6,3584]{2,1,0:T(8,128)(2,1)}), bf16[16,6,3584]{2,1,0:T(8,128)(2,1)S(1)}, u32[]{:S(2)}, u32[]{:S(2)}) async-start(bf16[16,6,3584]{2,1,0:T(8,128)(2,1)} %reshape.382), calls=%async_computation.3 | async-start | bytes 1835008 | tf_op jit(solution)/shard_map/all_to_all | solution.py:75
  328.7 22.2 %all-to-all-start.7 = ((bf16[16,6,3584]{2,1,0:T(8,128)(2,1)}), bf16[16,6,3584]{2,1,0:T(8,128)(2,1)S(1)}, u32[]{:S(2)}, u32[]{:S(2)}) async-start(bf16[16,6,3584]{2,1,0:T(8,128)(2,1)} %reshape.390), calls=%async_computation.7 | async-start | bytes 1835008 | tf_op jit(solution)/shard_map/all_to_all | solution.py:75
Sparse Core Ops, SparseCore 0:
  9.9 20.8 all-gather.4
  32.5 19.5 all-gather.6
  181.6 14.7 reduce-scatter.2
  199.0 22.3 reduce-scatter.4
where the time goes:
time: 369 us; the launch traced here: 366 us
  blocking collectives  113 us (31%)
  waiting for transfers between devices  110 us (30%)
  local copies, waits for them, and re-layouts  42.3 us (11%)
  starting transfers between devices  40.4 us (11%)
  matrix products  34.7 us (9%)
  between operations  14.5 us (4%)
  other arithmetic  11.2 us (3%)
    all_to_all x3, blocking collectives, deliver(): lax.all_to_all(sending, 'expert', split_axis=1, concat_axis=1, tiled=True)  113 us
    all_to_all x4, waiting for transfers between devices, collect(): lax.all_to_all(partial_value, 'expert', split_axis=0, concat_axis=0, tile...  76 us
    all_to_all x1, waiting for transfers between devices, deliver(): lax.all_to_all(sending, 'expert', split_axis=1, concat_axis=1, tiled=True)  22.5 us
    all_to_all x4, starting transfers between devices, collect(): lax.all_to_all(partial_value, 'expert', split_axis=0, concat_axis=0, tile...  18.5 us
    ppermute x2, starting transfers between devices, shifted(): return lax.ppermute(x, axis, pairs)  14.2 us
    slice x2, local copies, waits for them, and re-layouts, backward_pass(): inputs = arrived[0].reshape(-1, features)  13.2 us
    ppermute x2, waiting for transfers between devices, shifted(): return lax.ppermute(x, axis, pairs)  10.5 us
    dot_general x2, matrix products, forward_pass(): jnp.dot(hidden, down_full, preferred_element_type=jnp.float32)  10.3 us
  transfers between devices with their start and end apart: 11, of which 7 were waited for; matrix products, arithmetic and copies ran while one was open for 14% of the time, Pallas kernels for 0%

commit v1 on v0

v1 whole, which is shorter than its diff:
```python
import functools

import jax
import jax.numpy as jnp
import numpy as np
from jax import lax
from jax.experimental import pallas as pl
from jax.experimental.pallas import tpu as pltpu
from jax.sharding import PartitionSpec as P

MESH = pl.DeviceIdType.MESH
F32 = jnp.float32
BF16 = jnp.bfloat16
CAP = 6
QUARTERS = 4
SEMS = 140


def regroup_matrix():
    matrix = np.zeros((192, 192), np.float32)
    for z in range(4):
        for pair in range(2):
            for half in range(2):
                for part in range(2):
                    for slot in range(CAP):
                        row = (((pair * 2 + half) * 2 + part) * 4 + z) * CAP + slot
                        column = (((z * 2 + pair) * 2 + half) * 2 + part) * CAP + slot
                        matrix[row, column] = 1.0
    return matrix


def silu_slope(values):
    logistic = jax.nn.sigmoid(values)
    return logistic * (1.0 + values * (1.0 - logistic))


def dot(left, right, dims=((1,), (0,))):
    return lax.dot_general(left, right, (dims, ((), ())), preferred_element_type=F32)


def kernel(
    sections,
    width,
    hidden,
    act_hbm,
    fresh_hbm,
    grad_hbm,
    fresh_grad_hbm,
    saved_hbm,
    up_hbm,
    down_hbm,
    place_ref,
    gate_ref,
    regroup_ref,
    regroup_back_ref,
    acts_out,
    grads_out,
    up_out,
    down_out,
    act,
    fresh,
    grad,
    fresh_grad,
    saved,
    up,
    down,
    select,
    folded,
    z_send,
    z_got,
    z_pass,
    row_send,
    row_got,
    inputs,
    dp_send,
    dp_got,
    hid_kept,
    pre_kept,
    part_own,
    part_send,
    part_got,
    back_send,
    back_got,
    mixed,
    relayed,
    acts_buf,
    grads_buf,
    up_buf,
    down_buf,
    send_sems,
    recv_sems,
    local_sems,
):
    half_width = 2 * width
    section = lax.axis_index("pipe")
    owner = lax.axis_index("expert")
    core = lax.axis_index("dp")
    z = owner // 4
    x = owner % 4
    pair = x // 2
    partner = z * 4 + (x // 2) * 2 + (1 - x % 2)
    across = z * 4 + (3 - x)
    above = ((z + 1) % 4) * 4 + x
    below = ((z + 3) % 4) * 4 + x
    long_to = ((z + 1 + 2 * core) % 4) * 4 + x
    short_to = ((z + 3 - 2 * core) % 4) * 4 + x
    other = 1 - core
    ahead = (section + 1) % sections
    behind = (section + sections - 1) % sections

    loads = {}

    def load(name, source, target, index):
        loads[name] = pltpu.make_async_copy(source, target, local_sems.at[index])
        loads[name].start()

    load("act", act_hbm, act, 0)
    load("saved", saved_hbm, saved, 1)
    load("grad", grad_hbm, grad, 2)
    load("up", up_hbm, up, 3)
    load("down", down_hbm, down, 4)
    load("fresh", fresh_hbm, fresh, 5)
    load("fresh_grad", fresh_grad_hbm, fresh_grad, 6)

    barrier = pltpu.get_barrier_semaphore()
    peers = [{"dp": other}]
    for side in range(2):
        peers.append({"expert": partner, "dp": side})
        peers.append({"expert": across, "dp": side})
    peers += [{"expert": above}, {"expert": below}, {"pipe": ahead}, {"pipe": behind}]
    if sections == 2:
        peers = peers[:-1]
    for peer in peers:
        pl.semaphore_signal(barrier, inc=1, device_id=peer, device_id_type=MESH)

    def selection(which):
        place = place_ref[which : which + 1, :]
        expert = place >> 3
        slot = place & 7
        lane = lax.broadcasted_iota(jnp.int32, (1, 128), 1)
        z_steps = ((expert >> 1) + 4 - z) & 3
        flipped = (expert & 1) ^ pair
        row = z_steps * 48 + flipped * 24 + (lane >> 5) * CAP + slot
        rows = lax.broadcasted_iota(jnp.int32, (192, 128), 0)
        select[which] = jnp.where(rows == row, 1.0, 0.0).astype(BF16)

    def gate_column(which):
        row = gate_ref[which : which + 1, :]
        diagonal = lax.broadcasted_iota(jnp.int32, (128, 128), 0) == lax.broadcasted_iota(
            jnp.int32, (128, 128), 1
        )
        return jnp.sum(jnp.where(diagonal, row, 0.0), axis=1, keepdims=True)

    copies = []

    def remote(source, target, device):
        index = len(copies)
        copy = pltpu.make_async_remote_copy(
            src_ref=source,
            dst_ref=target,
            send_sem=send_sems.at[index],
            recv_sem=recv_sems.at[index],
            device_id=device,
            device_id_type=MESH,
        )
        copy.start()
        copies.append(copy)
        return copy

    def fold(values, slot):
        for quarter in range(QUARTERS):
            folded[slot, quarter * 32 : quarter * 32 + 32, :] = values[
                :, quarter * width : (quarter + 1) * width
            ]

    def z_start(e):
        return [
            remote(z_send.at[e, pl.ds(0, 48)], z_got.at[e, pl.ds(144, 48)], {"expert": above}),
            remote(z_send.at[e, pl.ds(96, 48)], z_got.at[e, pl.ds(48, 48)], {"expert": below}),
            remote(z_send.at[e, pl.ds(48, 32)], z_pass.at[e, pl.ds(0, 32)], {"expert": long_to}),
            remote(z_send.at[e, pl.ds(80, 16)], z_pass.at[e, pl.ds(32, 16)], {"expert": short_to}),
        ]

    def z_forward(e, started):
        started[2].wait_recv()
        started.append(
            remote(z_pass.at[e, pl.ds(0, 32)], z_got.at[e, pl.ds(96, 32)], {"expert": long_to})
        )
        started[3].wait_recv()
        started.append(
            remote(z_pass.at[e, pl.ds(32, 16)], z_got.at[e, pl.ds(128, 16)], {"expert": short_to})
        )

    def z_finish(started):
        for item in (0, 1, 4, 5):
            started[item].wait_recv()

    def dispatch(u, which, slot):
        rows = dot(select[which], folded[slot]).astype(BF16)
        z_got[u, 0:48, :] = rows[0:48]
        z_send[u] = rows[48:192]
        return z_start(u)

    def spread(u, started):
        z_finish(started)
        rows = dot(regroup_ref[...], z_got[u]).astype(BF16)
        for item in range(4):
            row_send[u, item] = rows[48 * item : 48 * item + 48]
        row_got[u, core] = row_send[u, core]
        return [
            remote(row_send.at[u, 2 + core], row_got.at[u, 2 + core], {"expert": across}),
            remote(
                row_send.at[u, 2 + other], row_got.at[u, 2 + core], {"expert": across, "dp": other}
            ),
            remote(row_send.at[u, core], row_got.at[u, 4 + core], {"expert": partner}),
            remote(
                row_send.at[u, other], row_got.at[u, 4 + core], {"expert": partner, "dp": other}
            ),
            remote(row_send.at[u, other], row_got.at[u, core], {"dp": other}),
        ]

    def spread_forward(u, sent):
        sent[0].wait_recv()
        sent.append(
            remote(row_got.at[u, 2 + core], row_got.at[u, 6 + core], {"expert": partner})
        )
        sent[1].wait_recv()
        sent.append(
            remote(row_got.at[u, 2 + other], row_got.at[u, 6 + other], {"expert": partner})
        )

    def gather(u, sent, place):
        for item in range(2, 7):
            sent[item].wait_recv()
        for both in range(4):
            first = row_got[u, 2 * both].astype(F32)
            second = row_got[u, 2 * both + 1].astype(F32)
            start = 192 * place + 48 * both
            for part in range(2):
                rows = jnp.concatenate(
                    [first[24 * part : 24 * part + 24], second[24 * part : 24 * part + 24]], axis=0
                )
                inputs[start : start + 48, part * width : (part + 1) * width] = rows.astype(BF16)

    def unit_rows(place):
        return inputs[192 * place : 192 * place + 192, :]

    def share_sum(item, partial_sum):
        dp_send[item] = partial_sum
        return remote(dp_send.at[item], dp_got.at[item], {"dp": other})

    def full_sum(item, copy):
        copy.wait_recv()
        return dp_send[item] + dp_got[item]

    def halves_start(c, product):
        part_send[c] = product(96).astype(BF16)
        copy = remote(part_send.at[c], part_got.at[c], {"expert": partner})
        part_own[c] = product(0).astype(BF16)
        return copy

    def halves_sum(c, copy):
        copy.wait_recv()
        for item in (2, 3, 0, 1):
            total = part_own[c, 48 * (item // 2) : 48 * (item // 2) + 48].astype(F32)
            total = total + part_got[c, 48 * (item // 2) : 48 * (item // 2) + 48].astype(F32)
            total = total[24 * (item % 2) : 24 * (item % 2) + 24]
            back_send[c, item] = jnp.concatenate(
                [total[:, :width], total[:, width:]], axis=0
            ).astype(BF16)
        back_got[c, core] = back_send[c, core]
        return [
            remote(back_send.at[c, 2 + core], back_got.at[c, 2 + core], {"expert": across}),
            remote(
                back_send.at[c, 2 + other],
                back_got.at[c, 2 + core],
                {"expert": across, "dp": other},
            ),
            remote(back_send.at[c, other], back_got.at[c, core], {"dp": other}),
        ]

    def returning(c, sent):
        for copy in sent:
            copy.wait_recv()
        gathered = jnp.concatenate([back_got[c, item] for item in range(4)], axis=0)
        rows = dot(regroup_back_ref[...], gathered).astype(BF16)
        z_got[6 + c, 0:48, :] = rows[0:48]
        z_send[6 + c] = rows[48:192]
        return z_start(6 + c)

    def mix(c, which, slot, gated, started):
        z_finish(started)
        picked = dot(select[which], z_got[6 + c], ((0,), (0,)))
        if gated:
            picked = gate_column(which) * picked
        mixed[c] = (folded[slot].astype(F32) + picked).astype(BF16)

    def give_out(c, buffer, target, which, index):
        for quarter in range(QUARTERS):
            buffer[which, :, quarter * width : (quarter + 1) * width] = mixed[
                c, quarter * 32 : quarter * 32 + 32, :
            ]
        copy = pltpu.make_async_copy(buffer.at[which], target.at[which], local_sems.at[index])
        copy.start()
        return copy

    def gate_folded(which, source, target):
        folded[target] = (gate_column(which) * folded[source].astype(F32)).astype(BF16)

    def forward_up(item, place):
        return share_sum(item, dot(unit_rows(place), up[...]))

    def forward_down(c, item, copy):
        active = jax.nn.silu(full_sum(item, copy)).astype(BF16)
        return halves_start(c, lambda start: dot(active[start : start + 96], down[...]))

    def grad_down(item, place):
        return share_sum(item, dot(unit_rows(place), down[...], ((1,), (1,))))

    def backward_up(c, step, items, sums):
        projected = full_sum(items[0], sums[0])
        rows = slice(192 * step, 192 * step + 192)
        hid_kept[rows] = jax.nn.silu(projected).astype(BF16)
        slope = silu_slope(projected)
        pre_grad = (full_sum(items[1], sums[1]) * slope).astype(BF16)
        pre_kept[rows] = pre_grad
        return halves_start(
            c, lambda start: dot(pre_grad[start : start + 96], up[...], ((1,), (1,)))
        )

    selection(0)
    loads["act"].wait()
    fold(act, 0)
    pl.semaphore_wait(barrier, len(peers))
    z0 = dispatch(0, 0, 0)
    selection(2)
    loads["saved"].wait()
    fold(saved.at[0], 1)
    z1 = dispatch(1, 2, 1)
    loads["grad"].wait()
    fold(grad, 6)
    gate_folded(2, 6, 2)
    z2 = dispatch(2, 2, 2)
    selection(1)
    selection(3)
    fold(saved.at[1], 3)
    z_forward(0, z0)
    r0 = spread(0, z0)
    z_forward(1, z1)
    spread_forward(0, r0)
    r1 = spread(1, z1)
    z_forward(2, z2)
    loads["up"].wait()
    loads["down"].wait()
    gather(0, r0, 4)
    d0 = forward_up(0, 4)
    spread_forward(1, r1)
    r2 = spread(2, z2)
    p0 = forward_down(0, 0, d0)
    z3 = dispatch(3, 3, 3)
    spread_forward(2, r2)
    gather(1, r1, 0)
    d1 = forward_up(1, 0)
    b0 = halves_sum(0, p0)
    gather(2, r2, 2)
    d2 = grad_down(2, 2)
    y0 = returning(0, b0)
    p1 = backward_up(1, 0, (1, 2), (d1, d2))
    z_forward(6, y0)
    z_forward(3, z3)
    loads["fresh"].wait()
    loads["fresh_grad"].wait()
    mix(0, 0, 0, True, y0)
    up_copy = remote(mixed.at[0], relayed.at[0], {"pipe": ahead})
    b1 = halves_sum(1, p1)
    out0 = give_out(0, acts_buf, acts_out, 0, 7)
    y1 = returning(1, b1)
    r3 = spread(3, z3)
    fold(fresh, 4)
    up_copy.wait_recv()
    folded[4] = jnp.where(section == 0, folded[4], relayed[0])
    z4 = dispatch(4, 1, 4)
    z_forward(7, y1)
    mix(1, 2, 6, False, y1)
    down_copy = remote(mixed.at[1], relayed.at[1], {"pipe": behind})
    out1 = give_out(1, grads_buf, grads_out, 0, 8)
    fold(fresh_grad, 7)
    z_forward(4, z4)
    spread_forward(3, r3)
    r4 = spread(4, z4)
    down_copy.wait_recv()
    folded[7] = jnp.where(section == sections - 1, folded[7], relayed[1])
    gate_folded(3, 7, 5)
    z5 = dispatch(5, 3, 5)
    spread_forward(4, r4)
    gather(3, r3, 1)
    d4 = forward_up(4, 1)
    z_forward(5, z5)
    gather(4, r4, 5)
    d3 = forward_up(3, 5)
    r5 = spread(5, z5)
    p2 = forward_down(2, 3, d3)
    spread_forward(5, r5)
    b2 = halves_sum(2, p2)
    gather(5, r5, 3)
    d5 = grad_down(5, 3)
    y2 = returning(2, b2)
    p3 = backward_up(3, 1, (4, 5), (d4, d5))
    z_forward(8, y2)

    def up_tile(step, carry):
        start = pl.multiple_of(step * 256, 256)
        up_buf[pl.ds(start, 256), :] = dot(
            inputs[0:384, pl.ds(start, 256)], pre_kept[...], ((0,), (0,))
        ).astype(BF16)
        return carry

    lax.fori_loop(0, half_width // 256, up_tile, 0)
    out_up = pltpu.make_async_copy(up_buf, up_out, local_sems.at[11])
    out_up.start()
    b3 = halves_sum(3, p3)
    mix(2, 1, 4, True, y2)
    out2 = give_out(2, acts_buf, acts_out, 1, 9)
    y3 = returning(3, b3)
    for part in range(2):
        columns = slice(part * width, (part + 1) * width)
        down_buf[:, columns] = dot(hid_kept[...], inputs[384:768, columns], ((0,), (0,))).astype(
            BF16
        )
    out_down = pltpu.make_async_copy(down_buf, down_out, local_sems.at[12])
    out_down.start()
    z_forward(9, y3)
    mix(3, 3, 7, False, y3)
    out3 = give_out(3, grads_buf, grads_out, 1, 10)
    for copy in copies:
        copy.wait_send()
    for copy in (out0, out1, out2, out3, out_up, out_down):
        copy.wait()
    assert len(copies) <= SEMS


def per_device(
    act_in,
    fresh_in,
    grad_in,
    fresh_grad,
    saved_input,
    expert_ids,
    slot_ids,
    gates,
    up_weight,
    down_weight,
):
    sections = lax.axis_size("pipe")
    tokens, features = fresh_in.shape
    width = features // QUARTERS
    hidden = up_weight.shape[2]
    place = jnp.tile(expert_ids[0, :, :, 0] * 8 + slot_ids[0, :, :, 0], (1, QUARTERS))
    gate_rows = jnp.tile(gates[0, :, :, 0], (1, QUARTERS))
    regroup = regroup_matrix()
    anywhere = pl.BlockSpec(memory_space=pl.ANY)
    in_vmem = pl.BlockSpec(memory_space=pltpu.VMEM)
    full = (tokens, features)
    vm = pltpu.VMEM
    acts, grads, up_grad, down_grad = pl.pallas_call(
        functools.partial(kernel, sections, width, hidden),
        out_shape=(
            jax.ShapeDtypeStruct((2,) + full, BF16),
            jax.ShapeDtypeStruct((2,) + full, BF16),
            jax.ShapeDtypeStruct((2 * width, hidden), BF16),
            jax.ShapeDtypeStruct((hidden, 2 * width), BF16),
        ),
        in_specs=[anywhere] * 7 + [in_vmem] * 4,
        out_specs=[anywhere] * 4,
        scratch_shapes=[
            vm(full, BF16),
            vm(full, BF16),
            vm(full, BF16),
            vm(full, BF16),
            vm((2,) + full, BF16),
            vm((2 * width, hidden), BF16),
            vm((hidden, 2 * width), BF16),
            vm((4, 192, 128), BF16),
            vm((8, 128, width), BF16),
            vm((10, 144, width), BF16),
            vm((10, 192, width), BF16),
            vm((10, 48, width), BF16),
            vm((6, 4, 48, width), BF16),
            vm((6, 8, 48, width), BF16),
            vm((1152, 2 * width), BF16),
            vm((6, 192, hidden), F32),
            vm((6, 192, hidden), F32),
            vm((384, hidden), BF16),
            vm((384, hidden), BF16),
            vm((4, 96, 2 * width), BF16),
            vm((4, 96, 2 * width), BF16),
            vm((4, 96, 2 * width), BF16),
            vm((4, 4, 48, width), BF16),
            vm((4, 4, 48, width), BF16),
            vm((4, 128, width), BF16),
            vm((2, 128, width), BF16),
            vm((2,) + full, BF16),
            vm((2,) + full, BF16),
            vm((2 * width, hidden), BF16),
            vm((hidden, 2 * width), BF16),
            pltpu.SemaphoreType.DMA((SEMS,)),
            pltpu.SemaphoreType.DMA((SEMS,)),
            pltpu.SemaphoreType.DMA((13,)),
        ],
        compiler_params=pltpu.CompilerParams(
            collective_id=0, has_side_effects=True, vmem_limit_bytes=60 * 2**20
        ),
    )(
        act_in[0],
        fresh_in,
        grad_in[0],
        fresh_grad,
        saved_input[:, 0],
        up_weight[0],
        down_weight[0],
        place,
        gate_rows,
        jnp.asarray(regroup, BF16),
        jnp.asarray(regroup.T, BF16),
    )
    return acts[:, None], grads[:, None], up_grad[None], down_grad[None]


def solution(mesh):
    in_specs = (
        P("pipe", ("expert", "dp"), None),
        P(("expert", "dp"), None),
        P("pipe", ("expert", "dp"), None),
        P(("expert", "dp"), None),
        P(None, "pipe", ("expert", "dp"), None),
        P("pipe", None, ("expert", "dp"), None),
        P("pipe", None, ("expert", "dp"), None),
        P("pipe", None, ("expert", "dp"), None),
        P("pipe", "dp", "expert"),
        P("pipe", "expert", "dp"),
    )
    out_specs = (
        P(None, "pipe", ("expert", "dp"), None),
        P(None, "pipe", ("expert", "dp"), None),
        P("pipe", "dp", "expert"),
        P("pipe", "expert", "dp"),
    )
    return jax.shard_map(
        per_device, mesh=mesh, in_specs=in_specs, out_specs=out_specs, check_vma=False
    )
```

time: 369 us -> 183 us (0.50)
  Pallas kernels: 0 us -> 170 us
  blocking collectives: 113 us -> 0 us
  waiting for transfers between devices: 110 us -> 0 us
  starting transfers between devices: 40.4 us -> 0 us
  matrix products: 34.7 us -> 0 us
  local copies, waits for them, and re-layouts: 42.3 us -> 9.17 us
  between operations: 14.5 us -> 0.65 us
  other arithmetic: 11.2 us -> 0.7 us
    pallas_call x0 -> x1, Pallas kernels: none -> 170 us  [per_device(): pl.pallas_call(functools.partial(kernel, sections, width, hidden), out_sh...]
    all_to_all x3 -> x0, blocking collectives: 113 us -> none  [deliver(): lax.all_to_all(sending, 'expert', split_axis=1, concat_axis=1, tiled=True)]
    all_to_all x5 -> x0, waiting for transfers between devices: 98.5 us -> none  [the longest x4 76 us: collect(): lax.all_to_all(partial_value, 'expert', split_axis=0, concat_axis=0, tile...]
    dot_general x10 -> x0, matrix products: 34.7 us -> none  [the longest x2 10.3 us: forward_pass(): jnp.dot(hidden, down_full, preferred_element_type=jnp.float32)]
    all_to_all x5 -> x0, starting transfers between devices: 25.8 us -> none  [the longest x4 18.5 us: collect(): lax.all_to_all(partial_value, 'expert', split_axis=0, concat_axis=0, tile...]
    ppermute x2 -> x0, starting transfers between devices: 14.2 us -> none  [shifted(): return lax.ppermute(x, axis, pairs)]
    slice x2 -> x0, local copies, waits for them, and re-layouts: 13.2 us -> none  [backward_pass(): inputs = arrived[0].reshape(-1, features)]
    ppermute x2 -> x0, waiting for transfers between devices: 10.5 us -> none  [shifted(): return lax.ppermute(x, axis, pairs)]
  transfers between devices with their start and end apart: 11 -> 0, of which waited for: 7 -> 0; matrix products, arithmetic and copies ran while one was open for 14% -> 0% of each run, Pallas kernels for 0% -> 0%
where the time goes in v1:
time: 183 us; the launch traced here: 181 us
  Pallas kernels  170 us (93%)
  local copies, waits for them, and re-layouts  9.17 us (5%)
    pallas_call x1, Pallas kernels, per_device(): pl.pallas_call(functools.partial(kernel, sections, width, hidden), out_sh...  170 us
    unnamed x8, local copies, waits for them, and re-layouts  7.16 us

profile of v1, /device:TPU:32, one launch (start us, length us, event | category | flops | bytes accessed | tf_op | source)
XLA Modules:
  0.0 180.7 jit_solution(8773216628934743648)
XLA Ops:
  0.6 0.7 multiply_add_fusion
  1.3 0.7 tile.20.place_ref
  2.0 0.7 tile.22
  2.7 0.7 tile.23.gate_ref
  3.4 170.1 %shard_map.147 = (bf16[2,32,3584]{2,1,0:T(8,128)(2,1)}, bf16[2,32,3584]{2,1,0:T(8,128)(2,1)}, bf16[1792,512]{1,0:T(8,128)(2,1)}, bf16[512,1792]{1,0:T(8,128)(2,1)}) custom-call(bf16[32,3584]{1,0:T(8,128)(2,1)} %bitcast.22, bf16[32,3584]{1,0:T(8,128)(2,1)} %fresh_hbm.1, bf16[32,3584]{1,0:T(8,128)(2,1)} %bitcast.23, bf16[32,3584]{1,0:T(8,128)(2,1)} %fresh_grad_hbm.1, ...), custom_call_target="tpu_custom_call" | custom-call | tf_op jit(solution)/shard_map/pallas_call | solution.py:465
  173.5 0.0 copy-start.1
  173.5 1.9 %copy.22 = bf16[2,1,32,3584]{3,2,1,0:T(8,128)(2,1)} copy(bf16[2,1,32,3584]{3,2,1,0:T(8,128)(2,1)} %bitcast.21) | data formatting | bytes 917504
  175.5 1.8 %copy.23 = bf16[2,1,32,3584]{3,2,1,0:T(8,128)(2,1)} copy(bf16[2,1,32,3584]{3,2,1,0:T(8,128)(2,1)} %bitcast.20) | data formatting | bytes 917504
  177.3 0.0 copy-done.1
  177.3 0.0 copy-start
  177.3 1.2 copy.24
  178.5 0.9 copy-done
  179.4 1.2 copy.25
  (1 shorter events, 0.0 us)
Async XLA Ops:
  173.5 3.8 %copy-start.1 = (bf16[1792,512]{1,0:T(8,128)(2,1)S(1)}, bf16[1792,512]{1,0:T(8,128)(2,1)}, u32[]{:S(2)}) copy-start(bf16[1792,512]{1,0:T(8,128)(2,1)} %get-tuple-element.10) | copy-start | bytes 5505028
  177.3 2.2 %copy-start = (bf16[512,1792]{1,0:T(8,128)(2,1)S(1)}, bf16[512,1792]{1,0:T(8,128)(2,1)}, u32[]{:S(2)}) copy-start(bf16[512,1792]{1,0:T(8,128)(2,1)} %get-tuple-element.11) | copy-start | bytes 5505028

commit v2 on v1

v2 whole, which is shorter than its diff:
```python
import functools

import jax
import jax.numpy as jnp
import numpy as np
from jax import lax
from jax.experimental import pallas as pl
from jax.experimental.pallas import tpu as pltpu
from jax.sharding import PartitionSpec as P

MESH = pl.DeviceIdType.MESH
F32 = jnp.float32
BF16 = jnp.bfloat16
CAP = 6
QUARTERS = 4
SEMS = 310
CHUNKS = 2


def regroup_matrix():
    matrix = np.zeros((192, 192), np.float32)
    for z in range(4):
        for pair in range(2):
            for half in range(2):
                for part in range(2):
                    for slot in range(CAP):
                        row = (((pair * 2 + half) * 2 + part) * 4 + z) * CAP + slot
                        column = (((z * 2 + pair) * 2 + half) * 2 + part) * CAP + slot
                        matrix[row, column] = 1.0
    return matrix


def silu_slope(values):
    logistic = jax.nn.sigmoid(values)
    return logistic * (1.0 + values * (1.0 - logistic))


def dot(left, right, dims=((1,), (0,))):
    return lax.dot_general(left, right, (dims, ((), ())), preferred_element_type=F32)


def kernel(
    sections,
    width,
    hidden,
    act_hbm,
    fresh_hbm,
    grad_hbm,
    fresh_grad_hbm,
    saved_hbm,
    up_hbm,
    down_hbm,
    place_ref,
    gate_ref,
    regroup_ref,
    regroup_back_ref,
    acts_out,
    grads_out,
    up_out,
    down_out,
    act,
    fresh,
    grad,
    fresh_grad,
    saved,
    up,
    down,
    select,
    folded,
    z_send,
    z_got,
    row_send,
    row_got,
    inputs,
    dp_send,
    dp_got,
    hid_kept,
    pre_kept,
    back_send,
    back_got,
    mixed,
    relayed,
    acts_buf,
    grads_buf,
    up_buf,
    down_buf,
    send_sems,
    recv_sems,
    local_sems,
):
    half_width = 2 * width
    section = lax.axis_index("pipe")
    owner = lax.axis_index("expert")
    core = lax.axis_index("dp")
    z = owner // 4
    x = owner % 4
    pair = x // 2
    partner = z * 4 + pair * 2 + (1 - x % 2)
    across = z * 4 + (3 - x)
    diagonal = z * 4 + (x + 2) % 4
    above = ((z + 1) % 4) * 4 + x
    below = ((z + 3) % 4) * 4 + x
    opposite = ((z + 2) % 4) * 4 + x
    other = 1 - core
    ahead = (section + 1) % sections
    behind = (section + sections - 1) % sections

    loads = {}

    def load(name, source, target, index):
        loads[name] = pltpu.make_async_copy(source, target, local_sems.at[index])
        loads[name].start()

    load("act", act_hbm, act, 0)
    load("saved", saved_hbm, saved, 1)
    load("grad", grad_hbm, grad, 2)
    load("up", up_hbm, up, 3)
    load("down", down_hbm, down, 4)
    load("fresh", fresh_hbm, fresh, 5)
    load("fresh_grad", fresh_grad_hbm, fresh_grad, 6)

    barrier = pltpu.get_barrier_semaphore()
    peers = [{"dp": other}]
    for owner_there in (partner, across, diagonal):
        peers.append({"expert": owner_there})
        peers.append({"expert": owner_there, "dp": other})
    for owner_there in (above, below, opposite):
        peers.append({"expert": owner_there})
    peers += [{"pipe": ahead}, {"pipe": behind}]
    if sections == 2:
        peers = peers[:-1]
    for peer in peers:
        pl.semaphore_signal(barrier, inc=1, device_id=peer, device_id_type=MESH)

    def selection(which):
        place = place_ref[which : which + 1, :]
        expert = place >> 3
        slot = place & 7
        lane = lax.broadcasted_iota(jnp.int32, (1, 128), 1)
        z_steps = ((expert >> 1) + 4 - z) & 3
        flipped = (expert & 1) ^ pair
        row = z_steps * 48 + flipped * 24 + (lane >> 5) * CAP + slot
        rows = lax.broadcasted_iota(jnp.int32, (192, 128), 0)
        select[which] = jnp.where(rows == row, 1.0, 0.0).astype(BF16)

    def gate_column(which):
        row = gate_ref[which : which + 1, :]
        on_diagonal = lax.broadcasted_iota(jnp.int32, (128, 128), 0) == lax.broadcasted_iota(
            jnp.int32, (128, 128), 1
        )
        return jnp.sum(jnp.where(on_diagonal, row, 0.0), axis=1, keepdims=True)

    copies = []

    def remote(source, target, device):
        index = len(copies)
        copy = pltpu.make_async_remote_copy(
            src_ref=source,
            dst_ref=target,
            send_sem=send_sems.at[index],
            recv_sem=recv_sems.at[index],
            device_id=device,
            device_id_type=MESH,
        )
        copy.start()
        copies.append(copy)
        return copy

    def fold(values, slot):
        for quarter in range(QUARTERS):
            folded[slot, quarter * 32 : quarter * 32 + 32, :] = values[
                :, quarter * width : (quarter + 1) * width
            ]

    def z_start(e, lanes):
        return [
            remote(
                z_send.at[e, pl.ds(start, 48), lanes],
                z_got.at[e, pl.ds(192 - 48 - start, 48), lanes],
                {"expert": device},
            )
            for start, device in ((48, opposite), (0, above), (96, below))
        ]

    def finish(started):
        for copy in started:
            copy.wait_recv()

    def span(lanes, part):
        return pl.ds(part * width + lanes.start, lanes.size)

    def dispatch(u, which, slot, lanes):
        rows = dot(select[which], folded[slot, :, lanes]).astype(BF16)
        z_got[u, 0:48, lanes] = rows[0:48]
        z_send[u, :, lanes] = rows[48:192]
        return z_start(u, lanes)

    def spread(u, started, lanes):
        finish(started)
        rows = dot(regroup_ref[...], z_got[u, :, lanes]).astype(BF16)
        for item in range(4):
            row_send[u, item, :, lanes] = rows[48 * item : 48 * item + 48]
        row_got[u, core, :, lanes] = row_send[u, core, :, lanes]

        def to(source, target, device):
            return remote(row_send.at[u, source, :, lanes], row_got.at[u, target, :, lanes], device)

        return [
            to(2 + core, 6 + core, {"expert": diagonal}),
            to(2 + other, 6 + core, {"expert": diagonal, "dp": other}),
            to(core, 4 + core, {"expert": partner}),
            to(other, 4 + core, {"expert": partner, "dp": other}),
            to(2 + core, 2 + core, {"expert": across}),
            to(2 + other, 2 + core, {"expert": across, "dp": other}),
            to(other, core, {"dp": other}),
        ]

    def gather(u, sent, place, lanes):
        finish(sent)
        for both in range(4):
            first = row_got[u, 2 * both, :, lanes].astype(F32)
            second = row_got[u, 2 * both + 1, :, lanes].astype(F32)
            start = 192 * place + 48 * both
            for part in range(2):
                rows = jnp.concatenate(
                    [first[24 * part : 24 * part + 24], second[24 * part : 24 * part + 24]], axis=0
                )
                inputs[start : start + 48, span(lanes, part)] = rows.astype(BF16)

    def times_up(place, lanes):
        rows = pl.ds(192 * place, 192)
        return sum(
            dot(inputs[rows, span(lanes, part)], up[span(lanes, part), :]) for part in range(2)
        )

    def times_down(place, lanes):
        rows = pl.ds(192 * place, 192)
        return sum(
            dot(inputs[rows, span(lanes, part)], down[:, span(lanes, part)], ((1,), (1,)))
            for part in range(2)
        )

    def share_sum(item, partial_sum):
        dp_send[item] = partial_sum
        return remote(dp_send.at[item], dp_got.at[item], {"dp": other})

    def full_sum(item, copy):
        copy.wait_recv()
        return dp_send[item] + dp_got[item]

    def give_back(c, product, lanes):
        parts = [product(span(lanes, part)) for part in range(2)]
        for item in (6, 7, 4, 5, 2, 3, 0, 1):
            rows = slice(24 * item, 24 * item + 24)
            back_send[c, item, :, lanes] = jnp.concatenate(
                [parts[0][rows], parts[1][rows]], axis=0
            ).astype(BF16)
        back_got[c, core, :, lanes] = back_send[c, core, :, lanes]

        def to(source, target, device):
            return remote(
                back_send.at[c, source, :, lanes], back_got.at[c, target, :, lanes], device
            )

        return [
            to(6 + core, 6 + core, {"expert": diagonal}),
            to(6 + other, 6 + core, {"expert": diagonal, "dp": other}),
            to(4 + core, 4 + core, {"expert": partner}),
            to(4 + other, 4 + core, {"expert": partner, "dp": other}),
            to(2 + core, 2 + core, {"expert": across}),
            to(2 + other, 2 + core, {"expert": across, "dp": other}),
            to(other, core, {"dp": other}),
        ]

    def returning(c, sent, lanes):
        finish(sent)
        totals = [
            (
                back_got[c, item, :, lanes].astype(F32) + back_got[c, item + 4, :, lanes].astype(F32)
            ).astype(BF16)
            for item in range(4)
        ]
        rows = dot(regroup_back_ref[...], jnp.concatenate(totals, axis=0)).astype(BF16)
        z_got[6 + c, 0:48, lanes] = rows[0:48]
        z_send[6 + c, :, lanes] = rows[48:192]
        return z_start(6 + c, lanes)

    def mix(c, which, slot, gated, started, lanes):
        finish(started)
        picked = dot(select[which], z_got[6 + c, :, lanes], ((0,), (0,)))
        if gated:
            picked = gate_column(which) * picked
        mixed[c, :, lanes] = (folded[slot, :, lanes].astype(F32) + picked).astype(BF16)

    def relay(item, device, lanes):
        return remote(mixed.at[item, :, lanes], relayed.at[item, :, lanes], {"pipe": device})

    def give_out(c, buffer, target, which, index):
        for quarter in range(QUARTERS):
            buffer[which, :, quarter * width : (quarter + 1) * width] = mixed[
                c, quarter * 32 : quarter * 32 + 32, :
            ]
        copy = pltpu.make_async_copy(buffer.at[which], target.at[which], local_sems.at[index])
        copy.start()
        return copy

    def gate_folded(which, source, target, lanes):
        folded[target, :, lanes] = (
            gate_column(which) * folded[source, :, lanes].astype(F32)
        ).astype(BF16)

    def receive(item, slot, at_end, copy, lanes):
        copy.wait_recv()
        folded[slot, :, lanes] = jnp.where(
            at_end, folded[slot, :, lanes], relayed[item, :, lanes]
        )

    groups = width // 128
    count = min(CHUNKS, groups)
    edges = [-(-groups * item // count) * 128 for item in range(count + 1)]
    chunks = [pl.ds(edges[item], edges[item + 1] - edges[item]) for item in range(count)]
    whole = pl.ds(0, width)
    every = range(count)

    selection(0)
    loads["act"].wait()
    fold(act, 0)
    pl.semaphore_wait(barrier, len(peers))
    z0 = [dispatch(0, 0, 0, lanes) for lanes in chunks]
    selection(2)
    loads["saved"].wait()
    fold(saved.at[0], 1)
    loads["grad"].wait()
    fold(grad, 6)
    gate_folded(2, 6, 2, whole)
    r0, r1, r2, r3, r4, r5 = [], [], [], [], [], []
    z1, z2, z3, z4, z5 = [], [], [], [], []
    for n in every:
        r0.append(spread(0, z0[n], chunks[n]))
        z1.append(dispatch(1, 2, 1, chunks[n]))
    selection(3)
    selection(1)
    fold(saved.at[1], 3)
    loads["up"].wait()
    loads["down"].wait()
    total = None
    for n in every:
        gather(0, r0[n], 4, chunks[n])
        product = times_up(4, chunks[n])
        total = product if total is None else total + product
        if n == count - 1:
            d0 = share_sum(0, total)
        r1.append(spread(1, z1[n], chunks[n]))
        z2.append(dispatch(2, 2, 2, chunks[n]))
    active = jax.nn.silu(full_sum(0, d0)).astype(BF16)
    p0 = [
        give_back(0, lambda columns: dot(active, down[:, columns]), lanes) for lanes in chunks
    ]
    for n in every:
        r2.append(spread(2, z2[n], chunks[n]))
        z3.append(dispatch(3, 3, 3, chunks[n]))
    total = None
    for lanes, copies_in in zip(chunks, r1):
        gather(1, copies_in, 0, lanes)
        product = times_up(0, lanes)
        total = product if total is None else total + product
    d1 = share_sum(1, total)
    y0 = [returning(0, p0[n], chunks[n]) for n in every]
    total = None
    for lanes, copies_in in zip(chunks, r2):
        gather(2, copies_in, 2, lanes)
        product = times_down(2, lanes)
        total = product if total is None else total + product
    d2 = share_sum(2, total)
    loads["fresh"].wait()
    loads["fresh_grad"].wait()
    fold(fresh, 4)
    fold(fresh_grad, 7)

    def backward_up(c, step, items, sums):
        projected = full_sum(items[0], sums[0])
        rows = slice(192 * step, 192 * step + 192)
        hid_kept[rows] = jax.nn.silu(projected).astype(BF16)
        slope = silu_slope(projected)
        pre_grad = (full_sum(items[1], sums[1]) * slope).astype(BF16)
        pre_kept[rows] = pre_grad
        return [
            give_back(c, lambda columns: dot(pre_grad, up[columns, :], ((1,), (1,))), lanes)
            for lanes in chunks
        ]

    p1 = backward_up(1, 0, (1, 2), (d1, d2))
    up_copies = []
    for n in every:
        mix(0, 0, 0, True, y0[n], chunks[n])
        up_copies.append(relay(0, ahead, chunks[n]))
    out0 = give_out(0, acts_buf, acts_out, 0, 7)
    y1 = [returning(1, p1[n], chunks[n]) for n in every]
    for n in every:
        receive(0, 4, section == 0, up_copies[n], chunks[n])
        z4.append(dispatch(4, 1, 4, chunks[n]))
    for n in every:
        r3.append(spread(3, z3[n], chunks[n]))
    down_copies = []
    for n in every:
        mix(1, 2, 6, False, y1[n], chunks[n])
        down_copies.append(relay(1, behind, chunks[n]))
    out1 = give_out(1, grads_buf, grads_out, 0, 8)
    for n in every:
        receive(1, 7, section == sections - 1, down_copies[n], chunks[n])
        gate_folded(3, 7, 5, chunks[n])
        z5.append(dispatch(5, 3, 5, chunks[n]))
    for n in every:
        r4.append(spread(4, z4[n], chunks[n]))
    total = None
    for lanes, copies_in in zip(chunks, r3):
        gather(3, copies_in, 1, lanes)
        product = times_up(1, lanes)
        total = product if total is None else total + product
    d4 = share_sum(4, total)
    total = None
    for n in every:
        gather(4, r4[n], 5, chunks[n])
        product = times_up(5, chunks[n])
        total = product if total is None else total + product
        if n == count - 1:
            d3 = share_sum(3, total)
        r5.append(spread(5, z5[n], chunks[n]))
    active_later = jax.nn.silu(full_sum(3, d3)).astype(BF16)
    p2 = [
        give_back(2, lambda columns: dot(active_later, down[:, columns]), lanes)
        for lanes in chunks
    ]
    total = None
    for lanes, copies_in in zip(chunks, r5):
        gather(5, copies_in, 3, lanes)
        product = times_down(3, lanes)
        total = product if total is None else total + product
    d5 = share_sum(5, total)
    y2 = [returning(2, p2[n], chunks[n]) for n in every]
    p3 = backward_up(3, 1, (4, 5), (d4, d5))

    def up_tile(step, carry):
        start = pl.multiple_of(step * 256, 256)
        up_buf[pl.ds(start, 256), :] = dot(
            inputs[0:384, pl.ds(start, 256)], pre_kept[...], ((0,), (0,))
        ).astype(BF16)
        return carry

    lax.fori_loop(0, half_width // 256, up_tile, 0)
    out_up = pltpu.make_async_copy(up_buf, up_out, local_sems.at[11])
    out_up.start()
    for n in every:
        mix(2, 1, 4, True, y2[n], chunks[n])
    out2 = give_out(2, acts_buf, acts_out, 1, 9)
    y3 = [returning(3, p3[n], chunks[n]) for n in every]
    for part in range(2):
        columns = slice(part * width, (part + 1) * width)
        down_buf[:, columns] = dot(hid_kept[...], inputs[384:768, columns], ((0,), (0,))).astype(
            BF16
        )
    out_down = pltpu.make_async_copy(down_buf, down_out, local_sems.at[12])
    out_down.start()
    for n in every:
        mix(3, 3, 7, False, y3[n], chunks[n])
    out3 = give_out(3, grads_buf, grads_out, 1, 10)
    for copy in copies:
        copy.wait_send()
    for copy in (out0, out1, out2, out3, out_up, out_down):
        copy.wait()
    assert len(copies) <= SEMS


def per_device(
    act_in,
    fresh_in,
    grad_in,
    fresh_grad,
    saved_input,
    expert_ids,
    slot_ids,
    gates,
    up_weight,
    down_weight,
):
    sections = lax.axis_size("pipe")
    tokens, features = fresh_in.shape
    width = features // QUARTERS
    hidden = up_weight.shape[2]
    place = jnp.tile(expert_ids[0, :, :, 0] * 8 + slot_ids[0, :, :, 0], (1, QUARTERS))
    gate_rows = jnp.tile(gates[0, :, :, 0], (1, QUARTERS))
    regroup = regroup_matrix()
    anywhere = pl.BlockSpec(memory_space=pl.ANY)
    in_vmem = pl.BlockSpec(memory_space=pltpu.VMEM)
    full = (tokens, features)
    vm = pltpu.VMEM
    acts, grads, up_grad, down_grad = pl.pallas_call(
        functools.partial(kernel, sections, width, hidden),
        out_shape=(
            jax.ShapeDtypeStruct((2,) + full, BF16),
            jax.ShapeDtypeStruct((2,) + full, BF16),
            jax.ShapeDtypeStruct((2 * width, hidden), BF16),
            jax.ShapeDtypeStruct((hidden, 2 * width), BF16),
        ),
        in_specs=[anywhere] * 7 + [in_vmem] * 4,
        out_specs=[anywhere] * 4,
        scratch_shapes=[
            vm(full, BF16),
            vm(full, BF16),
            vm(full, BF16),
            vm(full, BF16),
            vm((2,) + full, BF16),
            vm((2 * width, hidden), BF16),
            vm((hidden, 2 * width), BF16),
            vm((4, 192, 128), BF16),
            vm((8, 128, width), BF16),
            vm((10, 144, width), BF16),
            vm((10, 192, width), BF16),
            vm((6, 4, 48, width), BF16),
            vm((6, 8, 48, width), BF16),
            vm((1152, 2 * width), BF16),
            vm((6, 192, hidden), F32),
            vm((6, 192, hidden), F32),
            vm((384, hidden), BF16),
            vm((384, hidden), BF16),
            vm((4, 8, 48, width), BF16),
            vm((4, 8, 48, width), BF16),
            vm((4, 128, width), BF16),
            vm((2, 128, width), BF16),
            vm((2,) + full, BF16),
            vm((2,) + full, BF16),
            vm((2 * width, hidden), BF16),
            vm((hidden, 2 * width), BF16),
            pltpu.SemaphoreType.DMA((SEMS,)),
            pltpu.SemaphoreType.DMA((SEMS,)),
            pltpu.SemaphoreType.DMA((13,)),
        ],
        compiler_params=pltpu.CompilerParams(
            collective_id=0, has_side_effects=True, vmem_limit_bytes=60 * 2**20
        ),
    )(
        act_in[0],
        fresh_in,
        grad_in[0],
        fresh_grad,
        saved_input[:, 0],
        up_weight[0],
        down_weight[0],
        place,
        gate_rows,
        jnp.asarray(regroup, BF16),
        jnp.asarray(regroup.T, BF16),
    )
    return acts[:, None], grads[:, None], up_grad[None], down_grad[None]


def solution(mesh):
    in_specs = (
        P("pipe", ("expert", "dp"), None),
        P(("expert", "dp"), None),
        P("pipe", ("expert", "dp"), None),
        P(("expert", "dp"), None),
        P(None, "pipe", ("expert", "dp"), None),
        P("pipe", None, ("expert", "dp"), None),
        P("pipe", None, ("expert", "dp"), None),
        P("pipe", None, ("expert", "dp"), None),
        P("pipe", "dp", "expert"),
        P("pipe", "expert", "dp"),
    )
    out_specs = (
        P(None, "pipe", ("expert", "dp"), None),
        P(None, "pipe", ("expert", "dp"), None),
        P("pipe", "dp", "expert"),
        P("pipe", "expert", "dp"),
    )
    return jax.shard_map(
        per_device, mesh=mesh, in_specs=in_specs, out_specs=out_specs, check_vma=False
    )
```

time: 183 us -> 144 us (0.79)
  the two profiles are of different devices: /device:TPU:32 before, /device:TPU:25 now
where the time goes in v2:
time: 144 us
  Pallas kernels  133 us (92%)
  local copies, waits for them, and re-layouts  9.17 us (6%)
    pallas_call x1, Pallas kernels, per_device(): pl.pallas_call(functools.partial(kernel, sections, width, hidden), out_sh...  133 us
    unnamed x8, local copies, waits for them, and re-layouts  7.16 us

profile of v2, /device:TPU:25, one launch (start us, length us, event | category | flops | bytes accessed | tf_op | source)
XLA Modules:
  0.0 144.0 jit_solution(8055173931128318978)
XLA Ops:
  0.6 0.7 multiply_add_fusion
  1.3 0.7 tile.20.place_ref
  2.0 0.7 tile.22
  2.7 0.7 tile.23.gate_ref
  3.4 133.4 %shard_map.147 = (bf16[2,32,3584]{2,1,0:T(8,128)(2,1)}, bf16[2,32,3584]{2,1,0:T(8,128)(2,1)}, bf16[1792,512]{1,0:T(8,128)(2,1)}, bf16[512,1792]{1,0:T(8,128)(2,1)}) custom-call(bf16[32,3584]{1,0:T(8,128)(2,1)} %bitcast.22, bf16[32,3584]{1,0:T(8,128)(2,1)} %fresh_hbm.1, bf16[32,3584]{1,0:T(8,128)(2,1)} %bitcast.23, bf16[32,3584]{1,0:T(8,128)(2,1)} %fresh_grad_hbm.1, ...), custom_call_target="tpu_custom_call" | custom-call | tf_op jit(solution)/shard_map/pallas_call | solution.py:497
  136.8 0.0 copy-start.1
  136.8 1.9 %copy.22 = bf16[2,1,32,3584]{3,2,1,0:T(8,128)(2,1)} copy(bf16[2,1,32,3584]{3,2,1,0:T(8,128)(2,1)} %bitcast.21) | data formatting | bytes 917504
  138.8 1.8 %copy.23 = bf16[2,1,32,3584]{3,2,1,0:T(8,128)(2,1)} copy(bf16[2,1,32,3584]{3,2,1,0:T(8,128)(2,1)} %bitcast.20) | data formatting | bytes 917504
  140.6 0.0 copy-done.1
  140.6 0.0 copy-start
  140.6 1.2 copy.24
  141.8 0.9 copy-done
  142.7 1.2 copy.25
  (1 shorter events, 0.0 us)
Async XLA Ops:
  136.8 3.8 %copy-start.1 = (bf16[1792,512]{1,0:T(8,128)(2,1)S(1)}, bf16[1792,512]{1,0:T(8,128)(2,1)}, u32[]{:S(2)}) copy-start(bf16[1792,512]{1,0:T(8,128)(2,1)} %get-tuple-element.10) | copy-start | bytes 5505028
  140.6 2.2 %copy-start = (bf16[512,1792]{1,0:T(8,128)(2,1)S(1)}, bf16[512,1792]{1,0:T(8,128)(2,1)}, u32[]{:S(2)}) copy-start(bf16[512,1792]{1,0:T(8,128)(2,1)} %get-tuple-element.11) | copy-start | bytes 5505028

commit v3 on v2

--- a/solution.py
+++ b/solution.py
@@ -13,8 +13,33 @@
 BF16 = jnp.bfloat16
 CAP = 6
 QUARTERS = 4
-SEMS = 310
-CHUNKS = 2
+SEMS = 312
+CHUNKS = 3
+ORDER = (
+    ("D", 1, 2), ("D", 0, 2), ("D", 0, 1), ("D", 0, 0), ("S", 1, 2), ("D", 1, 0),
+    ("S", 0, 2), ("D", 2, 0), ("S", 0, 1), ("S", 0, 0), ("S", 1, 0), ("D", 2, 1),
+    ("D", 1, 1), ("D", 2, 2), ("S", 2, 0), ("G", 0, 0), ("G", 0, 1), ("G", 0, 2),
+    ("D", 3, 2), ("R", 0, 0), ("S", 1, 1), ("G", 1, 0), ("G", 2, 0), ("D", 3, 0),
+    ("S", 2, 1), ("S", 2, 2), ("Y", 0, 0), ("G", 1, 1), ("R", 0, 1), ("D", 3, 1),
+    ("R", 0, 2), ("G", 1, 2), ("G", 2, 1), ("G", 2, 2), ("M", 0, 0), ("R", 1, 0),
+    ("Y", 0, 1), ("Y", 0, 2), ("D", 4, 0), ("S", 3, 2), ("R", 1, 1), ("M", 0, 1),
+    ("R", 1, 2), ("Y", 1, 0), ("Y", 1, 1), ("M", 0, 2), ("S", 4, 0), ("D", 4, 1),
+    ("M", 1, 0), ("S", 3, 1), ("Y", 1, 2), ("S", 3, 0), ("D", 4, 2), ("D", 5, 0),
+    ("S", 4, 1), ("M", 1, 1), ("M", 1, 2), ("S", 4, 2), ("D", 5, 1), ("D", 5, 2),
+    ("S", 5, 0), ("G", 3, 0), ("G", 4, 0), ("G", 4, 1), ("G", 4, 2), ("G", 3, 1),
+    ("S", 5, 1), ("S", 5, 2), ("G", 5, 0), ("R", 2, 0), ("G", 3, 2), ("G", 5, 1),
+    ("G", 5, 2), ("R", 2, 1), ("R", 2, 2), ("R", 3, 0), ("Y", 2, 0), ("Y", 2, 1),
+    ("Y", 2, 2), ("R", 3, 1), ("M", 2, 0), ("Y", 3, 0), ("R", 3, 2), ("Y", 3, 1),
+    ("Y", 3, 2), ("M", 2, 2), ("M", 2, 1), ("WD", 0, 0), ("M", 3, 0), ("WU", 0, 0),
+    ("M", 3, 1), ("M", 3, 2),
+)
+
+
+PASS_OF_UNIT = (0, 2, 2, 3, 1, 3)
+FOLD_OF_UNIT = (0, 1, 2, 3, 4, 5)
+PLACE_OF_UNIT = (4, 0, 2, 1, 5, 3)
+PASS_OF_COLLECT = (0, 2, 1, 3)
+KEPT_OF_COLLECT = (0, 6, 4, 7)
 
 
 def regroup_matrix():
@@ -74,6 +99,7 @@
     inputs,
     dp_send,
     dp_got,
+    active_kept,
     hid_kept,
     pre_kept,
     back_send,
@@ -240,12 +266,8 @@
             for part in range(2)
         )
 
-    def share_sum(item, partial_sum):
-        dp_send[item] = partial_sum
-        return remote(dp_send.at[item], dp_got.at[item], {"dp": other})
-
-    def full_sum(item, copy):
-        copy.wait_recv()
+    def full_sum(item):
+        shared[item].wait_recv()
         return dp_send[item] + dp_got[item]
 
     def give_back(c, product, lanes):
@@ -320,155 +342,157 @@
     edges = [-(-groups * item // count) * 128 for item in range(count + 1)]
     chunks = [pl.ds(edges[item], edges[item + 1] - edges[item]) for item in range(count)]
     whole = pl.ds(0, width)
-    every = range(count)
-
-    selection(0)
-    loads["act"].wait()
-    fold(act, 0)
+    last = count - 1
+    weighted = {}
+    shared, outputs = {}, []
+    started = {}
+    ready = set()
+
+    def prepare(unit):
+        if unit in ready:
+            return
+        ready.add(unit)
+        which = PASS_OF_UNIT[unit]
+        if ("select", which) not in ready:
+            ready.add(("select", which))
+            selection(which)
+        if unit == 0:
+            loads["act"].wait()
+            fold(act, 0)
+        elif unit == 1:
+            loads["saved"].wait()
+            fold(saved.at[0], 1)
+        elif unit == 2:
+            loads["grad"].wait()
+            fold(grad, 6)
+            gate_folded(2, 6, 2, whole)
+        elif unit == 3:
+            prepare(1)
+            fold(saved.at[1], 3)
+        elif unit == 4:
+            loads["fresh"].wait()
+            fold(fresh, 4)
+        else:
+            loads["fresh_grad"].wait()
+            fold(fresh_grad, 7)
+
+    def run_dispatch(unit, n, lanes):
+        prepare(unit)
+        if unit == 4:
+            receive(0, 4, section == 0, started["relay", 0, n], lanes)
+        if unit == 5:
+            receive(1, 7, section == sections - 1, started["relay", 1, n], lanes)
+            gate_folded(3, 7, 5, lanes)
+        return dispatch(unit, PASS_OF_UNIT[unit], FOLD_OF_UNIT[unit], lanes)
+
+    def run_spread(unit, n, lanes):
+        for item in range(6):
+            prepare(item)
+        return spread(unit, started["D", unit, n], lanes)
+
+    def run_gather(unit, n, lanes):
+        place = PLACE_OF_UNIT[unit]
+        gather(unit, started["S", unit, n], place, lanes)
+        name = "down" if unit in (2, 5) else "up"
+        if name not in ready:
+            ready.add(name)
+            loads[name].wait()
+        product = times_down(place, lanes) if unit in (2, 5) else times_up(place, lanes)
+        dp_send[unit] = product if n == 0 else dp_send[unit] + product
+        if n == last:
+            shared[unit] = remote(dp_send.at[unit], dp_got.at[unit], {"dp": other})
+
+    def run_results(c, n, lanes):
+        step = c // 2
+        rows = slice(192 * step, 192 * step + 192)
+        if c % 2 == 0:
+            if n == 0:
+                active_kept[rows] = jax.nn.silu(full_sum(4 * step)).astype(BF16)
+            if "down" not in ready:
+                ready.add("down")
+                loads["down"].wait()
+            return give_back(c, lambda columns: dot(active_kept[rows], down[:, columns]), lanes)
+        if n == 0:
+            projected = full_sum(1 + 2 * step)
+            hid_kept[rows] = jax.nn.silu(projected).astype(BF16)
+            slope = silu_slope(projected)
+            pre_kept[rows] = (full_sum(2 + 3 * step) * slope).astype(BF16)
+        return give_back(
+            c, lambda columns: dot(pre_kept[rows], up[columns, :], ((1,), (1,))), lanes
+        )
+
+    def run_return(c, n, lanes):
+        return returning(c, started["R", c, n], lanes)
+
+    def run_mix(c, n, lanes):
+        mix(c, PASS_OF_COLLECT[c], KEPT_OF_COLLECT[c], c % 2 == 0, started["Y", c, n], lanes)
+        if c < 2:
+            started["relay", c, n] = relay(c, ahead if c == 0 else behind, lanes)
+        weighted[c] = weighted.get(c, 0) + 1
+        if weighted[c] == count:
+            buffer, target = ((acts_buf, acts_out), (grads_buf, grads_out))[c % 2]
+            outputs.append(give_out(c, buffer, target, c // 2, 7 + c))
+
+    def run_up_grad(unit, n, lanes):
+        def up_tile(step, carry):
+            start = pl.multiple_of(step * 256, 256)
+            up_buf[pl.ds(start, 256), :] = dot(
+                inputs[0:384, pl.ds(start, 256)], pre_kept[...], ((0,), (0,))
+            ).astype(BF16)
+            return carry
+
+        lax.fori_loop(0, half_width // 256, up_tile, 0)
+        outputs.append(pltpu.make_async_copy(up_buf, up_out, local_sems.at[11]))
+        outputs[-1].start()
+
+    def run_down_grad(unit, n, lanes):
+        for part in range(2):
+            columns = slice(part * width, (part + 1) * width)
+            down_buf[:, columns] = dot(
+                hid_kept[...], inputs[384:768, columns], ((0,), (0,))
+            ).astype(BF16)
+        outputs.append(pltpu.make_async_copy(down_buf, down_out, local_sems.at[12]))
+        outputs[-1].start()
+
+    steps = {
+        "D": run_dispatch,
+        "S": run_spread,
+        "G": run_gather,
+        "R": run_results,
+        "Y": run_return,
+        "M": run_mix,
+        "WU": run_up_grad,
+        "WD": run_down_grad,
+    }
+    prepare(0)
     pl.semaphore_wait(barrier, len(peers))
-    z0 = [dispatch(0, 0, 0, lanes) for lanes in chunks]
-    selection(2)
-    loads["saved"].wait()
-    fold(saved.at[0], 1)
-    loads["grad"].wait()
-    fold(grad, 6)
-    gate_folded(2, 6, 2, whole)
-    r0, r1, r2, r3, r4, r5 = [], [], [], [], [], []
-    z1, z2, z3, z4, z5 = [], [], [], [], []
-    for n in every:
-        r0.append(spread(0, z0[n], chunks[n]))
-        z1.append(dispatch(1, 2, 1, chunks[n]))
-    selection(3)
-    selection(1)
-    fold(saved.at[1], 3)
-    loads["up"].wait()
-    loads["down"].wait()
-    total = None
-    for n in every:
-        gather(0, r0[n], 4, chunks[n])
-        product = times_up(4, chunks[n])
-        total = product if total is None else total + product
-        if n == count - 1:
-            d0 = share_sum(0, total)
-        r1.append(spread(1, z1[n], chunks[n]))
-        z2.append(dispatch(2, 2, 2, chunks[n]))
-    active = jax.nn.silu(full_sum(0, d0)).astype(BF16)
-    p0 = [
-        give_back(0, lambda columns: dot(active, down[:, columns]), lanes) for lanes in chunks
-    ]
-    for n in every:
-        r2.append(spread(2, z2[n], chunks[n]))
-        z3.append(dispatch(3, 3, 3, chunks[n]))
-    total = None
-    for lanes, copies_in in zip(chunks, r1):
-        gather(1, copies_in, 0, lanes)
-        product = times_up(0, lanes)
-        total = product if total is None else total + product
-    d1 = share_sum(1, total)
-    y0 = [returning(0, p0[n], chunks[n]) for n in every]
-    total = None
-    for lanes, copies_in in zip(chunks, r2):
-        gather(2, copies_in, 2, lanes)
-        product = times_down(2, lanes)
-        total = product if total is None else total + product
-    d2 = share_sum(2, total)
-    loads["fresh"].wait()
-    loads["fresh_grad"].wait()
-    fold(fresh, 4)
-    fold(fresh_grad, 7)
-
-    def backward_up(c, step, items, sums):
-        projected = full_sum(items[0], sums[0])
-        rows = slice(192 * step, 192 * step + 192)
-        hid_kept[rows] = jax.nn.silu(projected).astype(BF16)
-        slope = silu_slope(projected)
-        pre_grad = (full_sum(items[1], sums[1]) * slope).astype(BF16)
-        pre_kept[rows] = pre_grad
-        return [
-            give_back(c, lambda columns: dot(pre_grad, up[columns, :], ((1,), (1,))), lanes)
-            for lanes in chunks
-        ]
-
-    p1 = backward_up(1, 0, (1, 2), (d1, d2))
-    up_copies = []
-    for n in every:
-        mix(0, 0, 0, True, y0[n], chunks[n])
-        up_copies.append(relay(0, ahead, chunks[n]))
-    out0 = give_out(0, acts_buf, acts_out, 0, 7)
-    y1 = [returning(1, p1[n], chunks[n]) for n in every]
-    for n in every:
-        receive(0, 4, section == 0, up_copies[n], chunks[n])
-        z4.append(dispatch(4, 1, 4, chunks[n]))
-    for n in every:
-        r3.append(spread(3, z3[n], chunks[n]))
-    down_copies = []
-    for n in every:
-        mix(1, 2, 6, False, y1[n], chunks[n])
-        down_copies.append(relay(1, behind, chunks[n]))
-    out1 = give_out(1, grads_buf, grads_out, 0, 8)
-    for n in every:
-        receive(1, 7, section == sections - 1, down_copies[n], chunks[n])
-        gate_folded(3, 7, 5, chunks[n])
-        z5.append(dispatch(5, 3, 5, chunks[n]))
-    for n in every:
-        r4.append(spread(4, z4[n], chunks[n]))
-    total = None
-    for lanes, copies_in in zip(chunks, r3):
-        gather(3, copies_in, 1, lanes)
-        product = times_up(1, lanes)
-        total = product if total is None else total + product
-    d4 = share_sum(4, total)
-    total = None
-    for n in every:
-        gather(4, r4[n], 5, chunks[n])
-        product = times_up(5, chunks[n])
-        total = product if total is None else total + product
-        if n == count - 1:
-            d3 = share_sum(3, total)
-        r5.append(spread(5, z5[n], chunks[n]))
-    active_later = jax.nn.silu(full_sum(3, d3)).astype(BF16)
-    p2 = [
-        give_back(2, lambda columns: dot(active_later, down[:, columns]), lanes)
-        for lanes in chunks
-    ]
-    total = None
-    for lanes, copies_in in zip(chunks, r5):
-        gather(5, copies_in, 3, lanes)
-        product = times_down(3, lanes)
-        total = product if total is None else total + product
-    d5 = share_sum(5, total)
-    y2 = [returning(2, p2[n], chunks[n]) for n in every]
-    p3 = backward_up(3, 1, (4, 5), (d4, d5))
-
-    def up_tile(step, carry):
-        start = pl.multiple_of(step * 256, 256)
-        up_buf[pl.ds(start, 256), :] = dot(
-            inputs[0:384, pl.ds(start, 256)], pre_kept[...], ((0,), (0,))
-        ).astype(BF16)
-        return carry
-
-    lax.fori_loop(0, half_width // 256, up_tile, 0)
-    out_up = pltpu.make_async_copy(up_buf, up_out, local_sems.at[11])
-    out_up.start()
-    for n in every:
-        mix(2, 1, 4, True, y2[n], chunks[n])
-    out2 = give_out(2, acts_buf, acts_out, 1, 9)
-    y3 = [returning(3, p3[n], chunks[n]) for n in every]
-    for part in range(2):
-        columns = slice(part * width, (part + 1) * width)
-        down_buf[:, columns] = dot(hid_kept[...], inputs[384:768, columns], ((0,), (0,))).astype(
-            BF16
-        )
-    out_down = pltpu.make_async_copy(down_buf, down_out, local_sems.at[12])
-    out_down.start()
-    for n in every:
-        mix(3, 3, 7, False, y3[n], chunks[n])
-    out3 = give_out(3, grads_buf, grads_out, 1, 10)
+    for kind, unit, n in ORDER:
+        started[kind, unit, n] = steps[kind](unit, n, chunks[n])
     for copy in copies:
         copy.wait_send()
-    for copy in (out0, out1, out2, out3, out_up, out_down):
+    for copy in outputs:
         copy.wait()
     assert len(copies) <= SEMS
+
+
+def hand_over(*refs):
+    count = 4
+    sources, targets, held = refs[:4], refs[4:8], refs[8:12]
+    sems = refs[12]
+    arrive = [
+        pltpu.make_async_copy(sources[item], held[item], sems.at[item]) for item in range(count)
+    ]
+    leave = [
+        pltpu.make_async_copy(held[item], targets[item], sems.at[count + item])
+        for item in range(count)
+    ]
+    for copy in arrive:
+        copy.start()
+    for item in range(count):
+        arrive[item].wait()
+        leave[item].start()
+    for copy in leave:
+        copy.wait()
 
 
 def per_device(
@@ -523,6 +547,7 @@
             vm((6, 192, hidden), F32),
             vm((384, hidden), BF16),
             vm((384, hidden), BF16),
+            vm((384, hidden), BF16),
             vm((4, 8, 48, width), BF16),
             vm((4, 8, 48, width), BF16),
             vm((4, 128, width), BF16),
@@ -551,7 +576,16 @@
         jnp.asarray(regroup, BF16),
         jnp.asarray(regroup.T, BF16),
     )
-    return acts[:, None], grads[:, None], up_grad[None], down_grad[None]
+    results = (acts[:, None], grads[:, None], up_grad[None], down_grad[None])
+    return pl.pallas_call(
+        hand_over,
+        out_shape=tuple(jax.ShapeDtypeStruct(item.shape, item.dtype) for item in results),
+        in_specs=[anywhere] * 4,
+        out_specs=[anywhere] * 4,
+        scratch_shapes=[vm(item.shape, item.dtype) for item in results]
+        + [pltpu.SemaphoreType.DMA((8,))],
+        compiler_params=pltpu.CompilerParams(vmem_limit_bytes=60 * 2**20),
+    )(*results)
 
 
 def solution(mesh):

time: 144 us -> 128 us (0.89)
  the two profiles are of different devices: /device:TPU:25 before, /device:TPU:32 now
where the time goes in v3:
time: 128 us; the launch traced here: 126 us
  Pallas kernels  123 us (96%)
  local copies, waits for them, and re-layouts  2.01 us (2%)
    pallas_call x1, Pallas kernels, per_device(): pl.pallas_call(functools.partial(kernel, sections, width, hidden), out_sh...  119 us
    pallas_call x1, Pallas kernels, per_device(): pl.pallas_call(hand_over, out_shape=tuple((jax.ShapeDtypeStruct(item.shap...  3.97 us

profile of v3, /device:TPU:32, one launch (start us, length us, event | category | flops | bytes accessed | tf_op | source)
XLA Modules:
  0.0 126.3 jit_solution(15822246390004130163)
XLA Ops:
  0.6 0.7 multiply_add_fusion
  1.3 0.7 tile.20.place_ref
  2.0 0.7 tile.22
  2.7 0.7 tile.23.gate_ref
  3.4 118.8 %shard_map.147 = (bf16[2,32,3584]{2,1,0:T(8,128)(2,1)}, bf16[2,32,3584]{2,1,0:T(8,128)(2,1)}, bf16[1792,512]{1,0:T(8,128)(2,1)}, bf16[512,1792]{1,0:T(8,128)(2,1)}) custom-call(bf16[32,3584]{1,0:T(8,128)(2,1)} %bitcast.18, bf16[32,3584]{1,0:T(8,128)(2,1)} %fresh_hbm.1, bf16[32,3584]{1,0:T(8,128)(2,1)} %bitcast.19, bf16[32,3584]{1,0:T(8,128)(2,1)} %fresh_grad_hbm.1, ...), custom_call_target="tpu_custom_call" | custom-call | tf_op jit(solution)/shard_map/pallas_call | solution.py:521
  122.2 4.0 %shard_map.148 = (bf16[2,1,32,3584]{3,2,1,0:T(8,128)(2,1)}, bf16[2,1,32,3584]{3,2,1,0:T(8,128)(2,1)}, bf16[1,1792,512]{2,1,0:T(8,128)(2,1)}, bf16[1,512,1792]{2,1,0:T(8,128)(2,1)}) custom-call(bf16[2,1,32,3584]{3,2,1,0:T(8,128)(2,1)} %bitcast.16, bf16[2,1,32,3584]{3,2,1,0:T(8,128)(2,1)} %bitcast.17, bf16[1,1792,512]{2,1,0:T(8,128)(2,1)} %bitcast.11, ...), custom_call_target="tpu_custom_call" | custom-call | tf_op jit(solution)/shard_map/pallas_call | solution.py:580
  (1 shorter events, 0.0 us)

commit v4 on v3

--- a/solution.py
+++ b/solution.py
@@ -13,25 +13,25 @@
 BF16 = jnp.bfloat16
 CAP = 6
 QUARTERS = 4
-SEMS = 312
+SEMS = 314
 CHUNKS = 3
 ORDER = (
-    ("D", 1, 2), ("D", 0, 2), ("D", 0, 1), ("D", 0, 0), ("S", 1, 2), ("D", 1, 0),
-    ("S", 0, 2), ("D", 2, 0), ("S", 0, 1), ("S", 0, 0), ("S", 1, 0), ("D", 2, 1),
-    ("D", 1, 1), ("D", 2, 2), ("S", 2, 0), ("G", 0, 0), ("G", 0, 1), ("G", 0, 2),
-    ("D", 3, 2), ("R", 0, 0), ("S", 1, 1), ("G", 1, 0), ("G", 2, 0), ("D", 3, 0),
-    ("S", 2, 1), ("S", 2, 2), ("Y", 0, 0), ("G", 1, 1), ("R", 0, 1), ("D", 3, 1),
-    ("R", 0, 2), ("G", 1, 2), ("G", 2, 1), ("G", 2, 2), ("M", 0, 0), ("R", 1, 0),
-    ("Y", 0, 1), ("Y", 0, 2), ("D", 4, 0), ("S", 3, 2), ("R", 1, 1), ("M", 0, 1),
-    ("R", 1, 2), ("Y", 1, 0), ("Y", 1, 1), ("M", 0, 2), ("S", 4, 0), ("D", 4, 1),
-    ("M", 1, 0), ("S", 3, 1), ("Y", 1, 2), ("S", 3, 0), ("D", 4, 2), ("D", 5, 0),
-    ("S", 4, 1), ("M", 1, 1), ("M", 1, 2), ("S", 4, 2), ("D", 5, 1), ("D", 5, 2),
-    ("S", 5, 0), ("G", 3, 0), ("G", 4, 0), ("G", 4, 1), ("G", 4, 2), ("G", 3, 1),
-    ("S", 5, 1), ("S", 5, 2), ("G", 5, 0), ("R", 2, 0), ("G", 3, 2), ("G", 5, 1),
-    ("G", 5, 2), ("R", 2, 1), ("R", 2, 2), ("R", 3, 0), ("Y", 2, 0), ("Y", 2, 1),
-    ("Y", 2, 2), ("R", 3, 1), ("M", 2, 0), ("Y", 3, 0), ("R", 3, 2), ("Y", 3, 1),
-    ("Y", 3, 2), ("M", 2, 2), ("M", 2, 1), ("WD", 0, 0), ("M", 3, 0), ("WU", 0, 0),
-    ("M", 3, 1), ("M", 3, 2),
+    ("D", 2, 1), ("D", 2, 0), ("D", 1, 1), ("D", 2, 2), ("S", 2, 1), ("D", 0, 0),
+    ("S", 2, 0), ("D", 1, 0), ("S", 1, 1), ("S", 2, 2), ("D", 1, 2), ("S", 1, 0),
+    ("D", 0, 1), ("S", 0, 0), ("D", 0, 2), ("G", 2, 0), ("S", 1, 2), ("G", 1, 0),
+    ("S", 0, 1), ("D", 3, 0), ("G", 2, 1), ("D", 3, 1), ("G", 2, 2), ("S", 0, 2),
+    ("G", 1, 1), ("G", 1, 2), ("R", 1, 0), ("R", 1, 1), ("D", 3, 2), ("G", 0, 0),
+    ("G", 0, 1), ("G", 0, 2), ("R", 1, 2), ("Y", 1, 0), ("R", 0, 0), ("Y", 1, 1),
+    ("R", 0, 1), ("R", 0, 2), ("Y", 1, 2), ("Y", 0, 0), ("Y", 0, 1), ("S", 3, 0),
+    ("M", 1, 0), ("M", 1, 1), ("Y", 0, 2), ("M", 0, 0), ("D", 5, 0), ("S", 3, 2),
+    ("M", 1, 2), ("D", 4, 0), ("D", 5, 1), ("G", 3, 0), ("M", 0, 2), ("S", 3, 1),
+    ("M", 0, 1), ("S", 5, 0), ("D", 5, 2), ("S", 4, 0), ("G", 3, 1), ("D", 4, 1),
+    ("G", 3, 2), ("D", 4, 2), ("S", 5, 1), ("S", 5, 2), ("G", 5, 0), ("S", 4, 1),
+    ("G", 5, 1), ("S", 4, 2), ("G", 5, 2), ("R", 3, 0), ("R", 3, 1), ("R", 3, 2),
+    ("G", 4, 0), ("G", 4, 1), ("G", 4, 2), ("WD", 0, 0), ("R", 2, 0), ("Y", 3, 0),
+    ("Y", 3, 1), ("R", 2, 1), ("WU", 0, 0), ("R", 2, 2), ("Y", 3, 2), ("Y", 2, 0),
+    ("Y", 2, 1), ("Y", 2, 2), ("M", 3, 0), ("M", 3, 1), ("M", 2, 1), ("M", 2, 0),
+    ("M", 3, 2), ("M", 2, 2),
 )
 
 
@@ -75,8 +75,7 @@
     saved_hbm,
     up_hbm,
     down_hbm,
-    place_ref,
-    gate_ref,
+    table_ref,
     regroup_ref,
     regroup_back_ref,
     acts_out,
@@ -159,7 +158,8 @@
         pl.semaphore_signal(barrier, inc=1, device_id=peer, device_id_type=MESH)
 
     def selection(which):
-        place = place_ref[which : which + 1, :]
+        row = table_ref[which : which + 1, :]
+        place = jnp.concatenate([row] * QUARTERS, axis=1).astype(jnp.int32)
         expert = place >> 3
         slot = place & 7
         lane = lax.broadcasted_iota(jnp.int32, (1, 128), 1)
@@ -170,13 +170,14 @@
         select[which] = jnp.where(rows == row, 1.0, 0.0).astype(BF16)
 
     def gate_column(which):
-        row = gate_ref[which : which + 1, :]
+        row = jnp.concatenate([table_ref[4 + which : 5 + which, :]] * QUARTERS, axis=1)
         on_diagonal = lax.broadcasted_iota(jnp.int32, (128, 128), 0) == lax.broadcasted_iota(
             jnp.int32, (128, 128), 1
         )
         return jnp.sum(jnp.where(on_diagonal, row, 0.0), axis=1, keepdims=True)
 
     copies = []
+    relays = {}
 
     def remote(source, target, device):
         index = len(copies)
@@ -314,8 +315,20 @@
             picked = gate_column(which) * picked
         mixed[c, :, lanes] = (folded[slot, :, lanes].astype(F32) + picked).astype(BF16)
 
-    def relay(item, device, lanes):
-        return remote(mixed.at[item, :, lanes], relayed.at[item, :, lanes], {"pipe": device})
+    def relay(item, device, sends, lanes):
+        index = len(copies)
+        copy = pltpu.make_async_remote_copy(
+            src_ref=mixed.at[item, :, lanes],
+            dst_ref=relayed.at[item, :, lanes],
+            send_sem=send_sems.at[index],
+            recv_sem=recv_sems.at[index],
+            device_id={"pipe": device},
+            device_id_type=MESH,
+        )
+        pl.when(sends)(copy.start)
+        copies.append(copy)
+        relays[index] = sends
+        return copy
 
     def give_out(c, buffer, target, which, index):
         for quarter in range(QUARTERS):
@@ -332,14 +345,14 @@
         ).astype(BF16)
 
     def receive(item, slot, at_end, copy, lanes):
-        copy.wait_recv()
-        folded[slot, :, lanes] = jnp.where(
-            at_end, folded[slot, :, lanes], relayed[item, :, lanes]
-        )
+        @pl.when(jnp.logical_not(at_end))
+        def _():
+            copy.wait_recv()
+            folded[slot, :, lanes] = relayed[item, :, lanes]
 
     groups = width // 128
     count = min(CHUNKS, groups)
-    edges = [-(-groups * item // count) * 128 for item in range(count + 1)]
+    edges = [groups * item // count * 128 for item in range(count + 1)]
     chunks = [pl.ds(edges[item], edges[item + 1] - edges[item]) for item in range(count)]
     whole = pl.ds(0, width)
     last = count - 1
@@ -427,7 +440,9 @@
     def run_mix(c, n, lanes):
         mix(c, PASS_OF_COLLECT[c], KEPT_OF_COLLECT[c], c % 2 == 0, started["Y", c, n], lanes)
         if c < 2:
-            started["relay", c, n] = relay(c, ahead if c == 0 else behind, lanes)
+            device = ahead if c == 0 else behind
+            sends = section < sections - 1 if c == 0 else section > 0
+            started["relay", c, n] = relay(c, device, sends, lanes)
         weighted[c] = weighted.get(c, 0) + 1
         if weighted[c] == count:
             buffer, target = ((acts_buf, acts_out), (grads_buf, grads_out))[c % 2]
@@ -468,8 +483,11 @@
     pl.semaphore_wait(barrier, len(peers))
     for kind, unit, n in ORDER:
         started[kind, unit, n] = steps[kind](unit, n, chunks[n])
-    for copy in copies:
-        copy.wait_send()
+    for index, copy in enumerate(copies):
+        if index in relays:
+            pl.when(relays[index])(copy.wait_send)
+        else:
+            copy.wait_send()
     for copy in outputs:
         copy.wait()
     assert len(copies) <= SEMS
@@ -511,8 +529,8 @@
     tokens, features = fresh_in.shape
     width = features // QUARTERS
     hidden = up_weight.shape[2]
-    place = jnp.tile(expert_ids[0, :, :, 0] * 8 + slot_ids[0, :, :, 0], (1, QUARTERS))
-    gate_rows = jnp.tile(gates[0, :, :, 0], (1, QUARTERS))
+    place = (expert_ids * 8 + slot_ids).astype(F32)
+    table = jnp.concatenate([place, gates], axis=1).reshape(8, tokens)
     regroup = regroup_matrix()
     anywhere = pl.BlockSpec(memory_space=pl.ANY)
     in_vmem = pl.BlockSpec(memory_space=pltpu.VMEM)
@@ -526,7 +544,7 @@
             jax.ShapeDtypeStruct((2 * width, hidden), BF16),
             jax.ShapeDtypeStruct((hidden, 2 * width), BF16),
         ),
-        in_specs=[anywhere] * 7 + [in_vmem] * 4,
+        in_specs=[anywhere] * 7 + [in_vmem] * 3,
         out_specs=[anywhere] * 4,
         scratch_shapes=[
             vm(full, BF16),
@@ -571,8 +589,7 @@
         saved_input[:, 0],
         up_weight[0],
         down_weight[0],
-        place,
-        gate_rows,
+        table,
         jnp.asarray(regroup, BF16),
         jnp.asarray(regroup.T, BF16),
     )

time: 128 us -> 124 us (0.969); the launches traced: 126 us -> 124 us
  local copies, waits for them, and re-layouts: 2.01 us -> 0 us
  Pallas kernels: 123 us -> 121 us
  other arithmetic: 0.7 us -> 1.98 us
    another operation x4 -> x0, local copies, waits for them, and re-layouts: 2.01 us -> none  [the longest x2 1.35 us: per_device(): gate_rows = jnp.tile(gates[0, :, :, 0], (1, QUARTERS))]
    pallas_call x1, Pallas kernels: 119 us -> 117 us  [per_device(): pl.pallas_call(functools.partial(kernel, sections, width, hidden), out_sh...]
    reshape x0 -> x1, other arithmetic: none -> 1.28 us  [per_device(): table = jnp.concatenate([place, gates], axis=1).reshape(8, tokens)]
where the time goes in v4:
time: 124 us
  Pallas kernels  121 us (98%)
  other arithmetic  1.98 us (2%)
    pallas_call x1, Pallas kernels, per_device(): pl.pallas_call(functools.partial(kernel, sections, width, hidden), out_sh...  117 us
    pallas_call x1, Pallas kernels, per_device(): pl.pallas_call(hand_over, out_shape=tuple((jax.ShapeDtypeStruct(item.shap...  3.97 us

profile of v4, /device:TPU:32, one launch (start us, length us, event | category | flops | bytes accessed | tf_op | source)
XLA Modules:
  0.0 124.2 jit_solution(2499946303110138307)
XLA Ops:
  0.6 0.7 add_convert_fusion
  1.3 1.3 %maximum_bitcast_fusion.table_ref = f32[8,32]{1,0:T(8,128)} fusion(f32[1,4,32,1]{2,1,3,0:T(4,128)} %bitcast.25, f32[1,4,32,1]{2,1,3,0:T(4,128)S(1)} %add_convert_fusion), kind=kLoop, calls=%fused_computation | loop fusion | flops 256 | bytes 2048 | tf_op jit(solution)/shard_map/reshape | solution.py:533
  2.6 117.4 %shard_map.147 = (bf16[2,32,3584]{2,1,0:T(8,128)(2,1)}, bf16[2,32,3584]{2,1,0:T(8,128)(2,1)}, bf16[1792,512]{1,0:T(8,128)(2,1)}, bf16[512,1792]{1,0:T(8,128)(2,1)}) custom-call(bf16[32,3584]{1,0:T(8,128)(2,1)} %bitcast.21, bf16[32,3584]{1,0:T(8,128)(2,1)} %fresh_hbm.1, bf16[32,3584]{1,0:T(8,128)(2,1)} %bitcast.22, bf16[32,3584]{1,0:T(8,128)(2,1)} %fresh_grad_hbm.1, ...), custom_call_target="tpu_custom_call" | custom-call | tf_op jit(solution)/shard_map/pallas_call | solution.py:539
  120.0 4.0 %shard_map.148 = (bf16[2,1,32,3584]{3,2,1,0:T(8,128)(2,1)}, bf16[2,1,32,3584]{3,2,1,0:T(8,128)(2,1)}, bf16[1,1792,512]{2,1,0:T(8,128)(2,1)}, bf16[1,512,1792]{2,1,0:T(8,128)(2,1)}) custom-call(bf16[2,1,32,3584]{3,2,1,0:T(8,128)(2,1)} %bitcast.19, bf16[2,1,32,3584]{3,2,1,0:T(8,128)(2,1)} %bitcast.20, bf16[1,1792,512]{2,1,0:T(8,128)(2,1)} %bitcast.14, ...), custom_call_target="tpu_custom_call" | custom-call | tf_op jit(solution)/shard_map/pallas_call | solution.py:597

commit v5 on v4

--- a/solution.py
+++ b/solution.py
@@ -220,6 +220,8 @@
         rows = dot(select[which], folded[slot, :, lanes]).astype(BF16)
         z_got[u, 0:48, lanes] = rows[0:48]
         z_send[u, :, lanes] = rows[48:192]
+        if not copies:
+            pl.semaphore_wait(barrier, len(peers))
         return z_start(u, lanes)
 
     def spread(u, started, lanes):
@@ -479,8 +481,8 @@
         "WU": run_up_grad,
         "WD": run_down_grad,
     }
-    prepare(0)
-    pl.semaphore_wait(barrier, len(peers))
+    for _, unit, _ in ORDER[:2]:
+        prepare(unit)
     for kind, unit, n in ORDER:
         started[kind, unit, n] = steps[kind](unit, n, chunks[n])
     for index, copy in enumerate(copies):

time: 124 us -> 124 us (level)
  no operation moved by 1% of the time
where the time goes in v5:
time: 124 us; the launch traced here: 123 us
  Pallas kernels  121 us (98%)
  other arithmetic  1.98 us (2%)
    pallas_call x1, Pallas kernels, per_device(): pl.pallas_call(functools.partial(kernel, sections, width, hidden), out_sh...  117 us
    pallas_call x1, Pallas kernels, per_device(): pl.pallas_call(hand_over, out_shape=tuple((jax.ShapeDtypeStruct(item.shap...  3.97 us

profile of v5, /device:TPU:32, one launch (start us, length us, event | category | flops | bytes accessed | tf_op | source)
XLA Modules:
  0.0 123.4 jit_solution(18025054409597392078)
XLA Ops:
  0.6 0.7 add_convert_fusion
  1.3 1.3 %maximum_bitcast_fusion.table_ref = f32[8,32]{1,0:T(8,128)} fusion(f32[1,4,32,1]{2,1,3,0:T(4,128)} %bitcast.25, f32[1,4,32,1]{2,1,3,0:T(4,128)S(1)} %add_convert_fusion), kind=kLoop, calls=%fused_computation | loop fusion | flops 256 | bytes 2048 | tf_op jit(solution)/shard_map/reshape | solution.py:535
  2.6 116.7 %shard_map.147 = (bf16[2,32,3584]{2,1,0:T(8,128)(2,1)}, bf16[2,32,3584]{2,1,0:T(8,128)(2,1)}, bf16[1792,512]{1,0:T(8,128)(2,1)}, bf16[512,1792]{1,0:T(8,128)(2,1)}) custom-call(bf16[32,3584]{1,0:T(8,128)(2,1)} %bitcast.21, bf16[32,3584]{1,0:T(8,128)(2,1)} %fresh_hbm.1, bf16[32,3584]{1,0:T(8,128)(2,1)} %bitcast.22, bf16[32,3584]{1,0:T(8,128)(2,1)} %fresh_grad_hbm.1, ...), custom_call_target="tpu_custom_call" | custom-call | tf_op jit(solution)/shard_map/pallas_call | solution.py:541
  119.3 4.0 %shard_map.148 = (bf16[2,1,32,3584]{3,2,1,0:T(8,128)(2,1)}, bf16[2,1,32,3584]{3,2,1,0:T(8,128)(2,1)}, bf16[1,1792,512]{2,1,0:T(8,128)(2,1)}, bf16[1,512,1792]{2,1,0:T(8,128)(2,1)}) custom-call(bf16[2,1,32,3584]{3,2,1,0:T(8,128)(2,1)} %bitcast.19, bf16[2,1,32,3584]{3,2,1,0:T(8,128)(2,1)} %bitcast.20, bf16[1,1792,512]{2,1,0:T(8,128)(2,1)} %bitcast.14, ...), custom_call_target="tpu_custom_call" | custom-call | tf_op jit(solution)/shard_map/pallas_call | solution.py:599
